TPU v7x, 32 devices: a whole 2x2x4 slice. The times are simulated.
32 devices in a mesh: space: 8 (over z, y), scene: 4 (over x, core).
Axes of the slice: x: 2, y: 2, z: 4, core: 2. Of those that a mesh axis runs over, the one named last changes fastest.
Arguments:
- features: bfloat16 [4, 16, 8, 8, 8, 256], P('scene', 'space'), may hold values from -6 to 6
- cotangent: bfloat16 [4, 16, 8, 8, 8, 256], P('scene', 'space'), may hold values from -6 to 6
- weight: bfloat16 [27, 256, 256], replicated, may hold values from -0.078125 to 0.078125
- counts: int32 [4, 8], P('scene', 'space'), may hold values from 1 to 2, as said below
- neighbours: int32 [4, 16, 26], P('scene', 'space'), may hold values from -1 to 15, as said below
- occupancy: int32 [4, 16, 512], P('scene', 'space'), may hold values 0 or 1
Outputs:
- outputs: bfloat16 [4, 16, 8, 8, 8, 256], P('scene', 'space')
- input_grad: bfloat16 [4, 16, 8, 8, 8, 256], P('scene', 'space')
- weight_grad: float32 [27, 256, 256], P(None, 'space', 'scene')
Inputs may be any that keep to these rules, and one draw needn't show every extreme that they name: Slots p * 2 to p * 2 + 1 of a scene form partition p; its first counts[s, p] slots are live. In every scene some partition has exactly 2 live slots. `neighbours`: an entry is -1 or the slot number of a live brick of the same scene in the same partition or the partition next to it; only live bricks have entries other than -1. The lists are symmetric: if brick a names brick c in direction d, brick c names brick a in the opposite direction.
All inputs are finite; a program needn't handle non-finite values. No bound on the sum of `occupancy` on one device may be relied on, other than what follows from the above.
Results may differ from a plain program's by a relative error of at most 0.001.
Values may be sent and summed in bfloat16 or wider, within the bound.
A program may use at most 128 MiB of HBM per device.

v0:
```python
import jax
import jax.numpy as jnp
from jax import lax
from jax.sharding import PartitionSpec as P


def extended(cells, sides, width):
    for axis, dim in sides:
        count = lax.axis_size(axis)
        ends = count - 1
        head = lax.slice_in_dim(cells, 0, width, axis=dim)
        tail = lax.slice_in_dim(cells, cells.shape[dim] - width, cells.shape[dim], axis=dim)
        cells = jnp.concatenate(
            [
                lax.ppermute(tail, axis, [(i, (i + 1) % count) for i in range(ends)]),
                cells,
                lax.ppermute(head, axis, [((i + 1) % count, i) for i in range(ends)]),
            ],
            axis=dim,
        )
    return cells


def boundary(offset, extent):
    if offset < 0:
        return slice(extent - 1, extent)
    if offset == 0:
        return slice(0, extent)
    return slice(0, 1)


def assemble(window, lookup):
    extent = window.shape[1]
    layers = []
    for shift_x in (-1, 0, 1):
        strips = []
        for shift_y in (-1, 0, 1):
            blocks = []
            for shift_z in (-1, 0, 1):
                column = (shift_x + 1) * 9 + (shift_y + 1) * 3 + shift_z + 1
                corner = window[
                    :,
                    boundary(shift_x, extent),
                    boundary(shift_y, extent),
                    boundary(shift_z, extent),
                ]
                blocks.append(jnp.take(corner, lookup[:, column], axis=0))
            strips.append(jnp.concatenate(blocks, axis=3))
        layers.append(jnp.concatenate(strips, axis=2))
    return jnp.concatenate(layers, axis=1)


def offsets():
    return [
        (shift_x, shift_y, shift_z)
        for shift_x in (-1, 0, 1)
        for shift_y in (-1, 0, 1)
        for shift_z in (-1, 0, 1)
    ]


def window_rows(padded, offset_xyz, extent):
    shift_x, shift_y, shift_z = offset_xyz
    region = padded[
        :,
        1 + shift_x : 1 + shift_x + extent,
        1 + shift_y : 1 + shift_y + extent,
        1 + shift_z : 1 + shift_z + extent,
    ]
    return region.reshape(-1, padded.shape[-1])


def forward_conv(padded, weight, extent):
    summed = None
    for column, offset_xyz in enumerate(offsets()):
        product = jnp.dot(
            window_rows(padded, offset_xyz, extent),
            weight[column],
            preferred_element_type=jnp.float32,
        )
        summed = product if summed is None else summed + product
    return summed


def backward_conv(padded, weight, extent):
    summed = None
    for column, offset_xyz in enumerate(offsets()):
        product = lax.dot_general(
            window_rows(padded, offset_xyz, extent),
            weight[26 - column],
            (((1,), (1,)), ((), ())),
            preferred_element_type=jnp.float32,
        )
        summed = product if summed is None else summed + product
    return summed


def weight_terms(padded, grad_rows, extent):
    return jnp.stack(
        [
            lax.dot_general(
                window_rows(padded, offset_xyz, extent),
                grad_rows,
                (((0,), (0,)), ((), ())),
                preferred_element_type=jnp.float32,
            )
            for offset_xyz in offsets()
        ]
    )


def per_device(features, cotangent, weight, counts, neighbours, occupancy):
    local_feats = features[0]
    bricks_here = local_feats.shape[0]
    extent = local_feats.shape[1]
    channels = local_feats.shape[-1]
    slot_live = (jnp.arange(bricks_here, dtype=jnp.int32) < counts[0, 0]).astype(jnp.int32)
    active = (
        (occupancy[0] * slot_live[:, None])
        .reshape(bricks_here, extent, extent, extent, 1)
        .astype(jnp.bfloat16)
    )
    hidden = jnp.maximum(local_feats, 0) * active
    masked_grad = cotangent[0] * active
    first_id = (lax.axis_index("space") - 1) * bricks_here
    linked = neighbours[0]
    local_ids = jnp.where(linked >= 0, linked - first_id, 3 * bricks_here)
    centre = (bricks_here + jnp.arange(bricks_here, dtype=jnp.int32))[:, None]
    lookup = jnp.concatenate([local_ids[:, :13], centre, local_ids[:, 13:]], axis=1)
    blank_brick = jnp.zeros((1, extent, extent, extent, channels), jnp.bfloat16)
    wide_hidden = extended(hidden, (("space", 0),), bricks_here)
    padded_hidden = assemble(jnp.concatenate([wide_hidden, blank_brick], axis=0), lookup)
    conv_out = forward_conv(padded_hidden, weight, extent).reshape(local_feats.shape)
    outputs = ((local_feats.astype(jnp.float32) + conv_out) * active).astype(jnp.bfloat16)
    wide_grad = extended(masked_grad, (("space", 0),), bricks_here)
    padded_grad = assemble(jnp.concatenate([wide_grad, blank_brick], axis=0), lookup)
    hidden_grad = backward_conv(padded_grad, weight, extent).reshape(local_feats.shape)
    input_grad = (
        masked_grad.astype(jnp.float32) + active * (local_feats > 0) * hidden_grad
    ).astype(jnp.bfloat16)
    norm_scale = float(
        lax.axis_size("scene") * lax.axis_size("space") * bricks_here * extent * extent * extent
    ) ** (-0.5)
    grad_terms = weight_terms(padded_hidden, masked_grad.reshape(-1, channels), extent) * norm_scale
    across_scene = lax.psum_scatter(grad_terms, "scene", scatter_dimension=2, tiled=True)
    weight_grad = lax.psum_scatter(across_scene, "space", scatter_dimension=1, tiled=True)
    return (outputs[None], input_grad[None], weight_grad)


def solution(mesh):
    in_specs = (
        P("scene", "space", None, None, None, None),
        P("scene", "space", None, None, None, None),
        P(),
        P("scene", "space"),
        P("scene", "space", None),
        P("scene", "space", None),
    )
    out_specs = (
        P("scene", "space", None, None, None, None),
        P("scene", "space", None, None, None, None),
        P(None, "space", "scene"),
    )
    return jax.shard_map(
        per_device, mesh=mesh, in_specs=in_specs, out_specs=out_specs, check_vma=False
    )
```

profile of v0, /device:TPU:1, one launch (start us, length us, event | category | flops | bytes accessed | tf_op | source)
XLA Modules:
  0.0 399.5 jit_solution(9989844993608056167)
XLA Ops:
  9.8 2.8 bitcast_multiply_fusion
  12.7 1.3 collective-permute-start.3
  14.0 4.6 %collective-permute-start.2 = (bf16[2,8,8,8,256]{4,0,3,2,1:T(2,128)(2,1)S(1)}, bf16[2,8,8,8,256]{4,0,3,2,1:T(2,128)(2,1)S(1)}, u32[]{:S(2)}, u32[]{:S(2)}) collective-permute-start(bf16[2,8,8,8,256]{4,0,3,2,1:T(2,128)(2,1)S(1)} %get-tuple-element.165), channel_id=1, source_target_pairs={{0,4},{4,8},{8,12},{12,16},{16,20},{20,24},{24,28},{1,5},{5,9},{9,... | collective-permute-start | bytes 1572872 | tf_op jit(solution)/shard_map/ppermute | solution.py:15
  18.6 1.3 collective-permute-start.1
  19.9 4.9 %collective-permute-start = (bf16[2,8,8,8,256]{4,0,3,2,1:T(2,128)(2,1)S(1)}, bf16[2,8,8,8,256]{4,0,3,2,1:T(2,128)(2,1)S(1)}, u32[]{:S(2)}, u32[]{:S(2)}) collective-permute-start(bf16[2,8,8,8,256]{4,0,3,2,1:T(2,128)(2,1)S(1)} %get-tuple-element.166), channel_id=1, source_target_pairs={{0,4},{4,8},{8,12},{12,16},{16,20},{20,24},{24,28},{1,5},{5,9},{9,... | collective-permute-start | bytes 1572872 | tf_op jit(solution)/shard_map/ppermute | solution.py:15
  48.6 3.0 collective-permute-done.2
  51.7 11.2 %collective-permute-done = bf16[2,8,8,8,256]{4,0,3,2,1:T(2,128)(2,1)S(1)} collective-permute-done((bf16[2,8,8,8,256]{4,0,3,2,1:T(2,128)(2,1)S(1)}, bf16[2,8,8,8,256]{4,0,3,2,1:T(2,128)(2,1)S(1)}, u32[]{:S(2)}, u32[]{:S(2)}) %collective-permute-start) | collective-permute-done | bytes 524320 | tf_op jit(solution)/shard_map/ppermute | solution.py:15
  62.9 3.8 maximum_maximum_fusion.1
  69.1 1.7 copy.558
  74.9 2.0 gather_fusion.44
  79.0 1.6 gather_fusion.43
  80.6 1.3 gather_fusion.16
  83.5 1.3 gather_fusion.42
  84.7 1.3 gather_fusion.15
  86.1 1.3 gather_fusion.41
  87.4 1.3 gather_fusion.14
  88.7 2.2 gather_fusion.40
  92.7 1.4 copy.513
  95.1 1.4 copy.510
  96.5 1.4 copy.508
  97.8 1.4 copy.505
  100.2 1.4 copy.502
  101.6 1.4 copy.500
  103.0 1.9 gather_fusion.53
  104.9 1.9 gather_fusion.26
  110.9 1.9 gather_fusion.51
  112.8 1.9 gather_fusion.24
  116.3 1.4 gather_fusion.50
  121.0 1.3 gather_fusion.49
  122.5 1.4 gather_fusion.22
  132.2 1.3 gather_fusion.45
  133.5 1.3 gather_fusion.18
  137.9 1.5 gather_fusion.11
  144.4 1.4 gather_fusion.9
  146.7 1.4 gather_fusion.8
  148.0 1.4 gather_fusion.35
  150.2 1.4 gather_fusion.7
  153.0 1.4 gather_fusion.6
  154.4 1.4 gather_fusion.33
  156.5 1.4 gather_fusion.5
  161.6 1.4 gather_fusion.3
  164.5 1.4 gather_fusion.2
  165.9 1.4 gather_fusion.29
  168.0 1.4 gather_fusion.1
  170.9 1.4 gather_fusion
  172.2 1.4 gather_fusion.27
  174.9 1.6 maximum_maximum_fusion.9
  177.6 2.8 fusion.193
  180.4 1.4 fusion.197
  181.8 1.4 fusion.196
  183.8 1.7 maximum_maximum_fusion.7
  185.6 3.1 maximum_maximum_fusion.2
  202.3 3.6 maximum_maximum_fusion.3
  209.6 3.5 broadcast_multiply_fusion
  213.0 10.3 %copy.610 = f32[27,256,256]{1,0,2:T(8,128)} copy(f32[27,256,256]{2,1,0:T(8,128)} %broadcast_multiply_fusion) | data formatting | bytes 14155776 | tf_op jit(solution)/shard_map/mul | solution.py:144
  223.5 1.5 fusion.29
  225.0 1.4 convolution_add_fusion.25
  234.9 3.4 maximum_maximum_fusion.5
  242.9 2.0 fusion.28
  254.5 41.8 %reduce-scatter.3.cloned.1.call-done = f32[27,256,64]{1,0,2:T(8,128)} async-done(((f32[27,256,256]{1,0,2:T(8,128)}), f32[27,256,64]{1,0,2:T(8,128)}) %reduce-scatter.3.cloned.1.call-update) | async-done | bytes 1769488 | tf_op jit(solution)/shard_map/reduce_scatter | solution.py:145
  296.3 5.8 %copy.611 = f32[27,256,64]{2,0,1:T(8,128)} copy(f32[27,256,64]{1,0,2:T(8,128)} %reduce-scatter.3.cloned.1.call-done) | data formatting | bytes 3538944 | tf_op jit(solution)/shard_map/reduce_scatter | solution.py:145
  313.9 1.3 convolution_add_fusion.27
  317.4 73.0 %reduce-scatter.5.cloned.1.call-done = f32[27,32,64]{2,0,1:T(8,128)} async-done(((f32[27,256,64]{2,0,1:T(8,128)}), f32[27,32,64]{2,0,1:T(8,128)}) %reduce-scatter.5.cloned.1.call-update) | async-done | bytes 221200 | tf_op jit(solution)/shard_map/reduce_scatter | solution.py:146
  390.4 2.1 copy.613
  (512 shorter events, 131.4 us)
Async XLA Ops:
  7.2 289.1 %reduce-scatter.3.cloned.1.call-start = ((), (), s32[]{:S(2)}) async-start(), calls=%async_computation.2 | async-start | bytes 10485760 | tf_op jit(solution)/shard_map/reduce_scatter | solution.py:145
  9.8 56.9 %copy-start.38 = (bf16[2,8,8,8]{0,3,2,1:T(8,128)(2,1)}, bf16[2,8,8,8]{0,3,2,1:T(8,128)(2,1)S(1)}, u32[]{:S(2)}) copy-start(bf16[2,8,8,8]{0,3,2,1:T(8,128)(2,1)S(1)} %copy.498) | copy-start | bytes 6148
  12.7 54.1 %copy-start.27 = (bf16[2,8,8,8,256]{4,0,3,2,1:T(2,128)(2,1)}, bf16[2,8,8,8,256]{4,0,3,2,1:T(2,128)(2,1)S(1)}, u32[]{:S(2)}) copy-start(bf16[2,8,8,8,256]{4,0,3,2,1:T(2,128)(2,1)S(1)} %get-tuple-element.165) | copy-start | bytes 1572868
  12.7 35.9 %collective-permute-start.3 = (bf16[2,8,8,8,256]{4,0,3,2,1:T(2,128)(2,1)S(1)}, bf16[2,8,8,8,256]{4,0,3,2,1:T(2,128)(2,1)S(1)}, u32[]{:S(2)}, u32[]{:S(2)}) collective-permute-start(bf16[2,8,8,8,256]{4,0,3,2,1:T(2,128)(2,1)S(1)} %get-tuple-element.165), channel_id=1, source_target_pairs={{4,0},{8,4},{12,8},{16,12},{20,16},{24,20},{28,24},{5,1},{9,5},{13... | collective-permute-start | bytes 1572872 | tf_op jit(solution)/shard_map/ppermute | solution.py:17
  14.0 37.7 %collective-permute-start.2 = (bf16[2,8,8,8,256]{4,0,3,2,1:T(2,128)(2,1)S(1)}, bf16[2,8,8,8,256]{4,0,3,2,1:T(2,128)(2,1)S(1)}, u32[]{:S(2)}, u32[]{:S(2)}) collective-permute-start(bf16[2,8,8,8,256]{4,0,3,2,1:T(2,128)(2,1)S(1)} %get-tuple-element.165), channel_id=1, source_target_pairs={{0,4},{4,8},{8,12},{12,16},{16,20},{20,24},{24,28},{1,5},{5,9},{9,... | collective-permute-start | bytes 1572872 | tf_op jit(solution)/shard_map/ppermute | solution.py:15
  18.6 33.0 %collective-permute-start.1 = (bf16[2,8,8,8,256]{4,0,3,2,1:T(2,128)(2,1)S(1)}, bf16[2,8,8,8,256]{4,0,3,2,1:T(2,128)(2,1)S(1)}, u32[]{:S(2)}, u32[]{:S(2)}) collective-permute-start(bf16[2,8,8,8,256]{4,0,3,2,1:T(2,128)(2,1)S(1)} %get-tuple-element.166), channel_id=1, source_target_pairs={{4,0},{8,4},{12,8},{16,12},{20,16},{24,20},{28,24},{5,1},{9,5},{13... | collective-permute-start | bytes 1572872 | tf_op jit(solution)/shard_map/ppermute | solution.py:17
  19.9 43.0 %collective-permute-start = (bf16[2,8,8,8,256]{4,0,3,2,1:T(2,128)(2,1)S(1)}, bf16[2,8,8,8,256]{4,0,3,2,1:T(2,128)(2,1)S(1)}, u32[]{:S(2)}, u32[]{:S(2)}) collective-permute-start(bf16[2,8,8,8,256]{4,0,3,2,1:T(2,128)(2,1)S(1)} %get-tuple-element.166), channel_id=1, source_target_pairs={{0,4},{4,8},{8,12},{12,16},{16,20},{20,24},{24,28},{1,5},{5,9},{9,... | collective-permute-start | bytes 1572872 | tf_op jit(solution)/shard_map/ppermute | solution.py:15
  91.6 33.1 %copy-start.63 = (bf16[7,8,256]{2,0,1:T(8,128)(2,1)S(1)}, bf16[7,8,256]{2,0,1:T(8,128)(2,1)}, u32[]{:S(2)}) copy-start(bf16[7,8,256]{2,0,1:T(8,128)(2,1)} %get-tuple-element.242) | copy-start | bytes 86020
  91.6 38.0 %copy-start.62 = (bf16[7,8,256]{2,0,1:T(8,128)(2,1)S(1)}, bf16[7,8,256]{2,0,1:T(8,128)(2,1)}, u32[]{:S(2)}) copy-start(bf16[7,8,256]{2,0,1:T(8,128)(2,1)} %get-tuple-element.65) | copy-start | bytes 86020
  91.6 43.1 %copy-start.40 = (bf16[7,8,8,256]{3,0,2,1:T(8,128)(2,1)S(1)}, bf16[7,8,8,256]{3,0,2,1:T(8,128)(2,1)}, u32[]{:S(2)}) copy-start(bf16[7,8,8,256]{3,0,2,1:T(8,128)(2,1)} %get-tuple-element.81) | copy-start | bytes 688132
  92.7 51.7 %copy-start.60 = (bf16[7,8,256]{2,0,1:T(8,128)(2,1)S(1)}, bf16[7,8,256]{2,0,1:T(8,128)(2,1)}, u32[]{:S(2)}) copy-start(bf16[7,8,256]{2,0,1:T(8,128)(2,1)} %get-tuple-element.75) | copy-start | bytes 86020
  94.1 56.1 %copy-start.61 = (bf16[7,8,256]{2,0,1:T(8,128)(2,1)S(1)}, bf16[7,8,256]{2,0,1:T(8,128)(2,1)}, u32[]{:S(2)}) copy-start(bf16[7,8,256]{2,0,1:T(8,128)(2,1)} %get-tuple-element.67) | copy-start | bytes 86020
  94.1 62.4 %copy-start.59 = (bf16[7,8,256]{2,0,1:T(8,128)(2,1)S(1)}, bf16[7,8,256]{2,0,1:T(8,128)(2,1)}, u32[]{:S(2)}) copy-start(bf16[7,8,256]{2,0,1:T(8,128)(2,1)} %get-tuple-element.71) | copy-start | bytes 86020
  107.6 54.0 %copy-start.58 = (bf16[7,8,256]{2,0,1:T(8,128)(2,1)S(1)}, bf16[7,8,256]{2,0,1:T(8,128)(2,1)}, u32[]{:S(2)}) copy-start(bf16[7,8,256]{2,0,1:T(8,128)(2,1)} %get-tuple-element.72) | copy-start | bytes 86020
  116.3 51.7 %copy-start.57 = (bf16[7,8,256]{2,0,1:T(8,128)(2,1)S(1)}, bf16[7,8,256]{2,0,1:T(8,128)(2,1)}, u32[]{:S(2)}) copy-start(bf16[7,8,256]{2,0,1:T(8,128)(2,1)} %get-tuple-element.68) | copy-start | bytes 86020
  118.9 55.0 %copy-start.50 = (bf16[2,8,8,256]{3,2,1,0:T(8,128)(2,1)S(1)}, bf16[2,8,8,256]{3,2,1,0:T(8,128)(2,1)}, u32[]{:S(2)}) copy-start(bf16[2,8,8,256]{3,2,1,0:T(8,128)(2,1)} %gather_fusion.16) | copy-start | bytes 196612
  120.0 54.2 %copy-start.51 = (bf16[2,8,8,256]{3,2,1,0:T(8,128)(2,1)S(1)}, bf16[2,8,8,256]{3,2,1,0:T(8,128)(2,1)}, u32[]{:S(2)}) copy-start(bf16[2,8,8,256]{3,2,1,0:T(8,128)(2,1)} %gather_fusion.41) | copy-start | bytes 196612
  120.0 54.2 %copy-start.52 = (bf16[2,8,8,256]{3,2,1,0:T(8,128)(2,1)S(1)}, bf16[2,8,8,256]{3,2,1,0:T(8,128)(2,1)}, u32[]{:S(2)}) copy-start(bf16[2,8,8,256]{3,2,1,0:T(8,128)(2,1)} %gather_fusion.14) | copy-start | bytes 196612
  122.3 24.2 %copy-start.98 = (pred[2]{0:T(512)(128)(4,1)S(1)}, pred[2]{0:T(512)(128)(4,1)}, u32[]{:S(2)}) copy-start(pred[2]{0:T(512)(128)(4,1)} %get-tuple-element.231) | copy-start | bytes 10
  122.3 27.1 %copy-start.97 = (pred[2]{0:T(512)(128)(4,1)S(1)}, pred[2]{0:T(512)(128)(4,1)}, u32[]{:S(2)}) copy-start(pred[2]{0:T(512)(128)(4,1)} %get-tuple-element.232) | copy-start | bytes 10
  122.3 30.0 %copy-start.117 = (pred[2]{0:T(512)(128)(4,1)S(1)}, pred[2]{0:T(512)(128)(4,1)}, u32[]{:S(2)}) copy-start(pred[2]{0:T(512)(128)(4,1)} %compare_and_fusion.19) | copy-start | bytes 10
  122.3 33.5 %copy-start.96 = (pred[2]{0:T(512)(128)(4,1)S(1)}, pred[2]{0:T(512)(128)(4,1)}, u32[]{:S(2)}) copy-start(pred[2]{0:T(512)(128)(4,1)} %get-tuple-element.267) | copy-start | bytes 10
  122.3 36.3 %copy-start.95 = (pred[2]{0:T(512)(128)(4,1)S(1)}, pred[2]{0:T(512)(128)(4,1)}, u32[]{:S(2)}) copy-start(pred[2]{0:T(512)(128)(4,1)} %get-tuple-element.268) | copy-start | bytes 10
  122.3 38.5 %copy-start.91 = (pred[2]{0:T(512)(128)(4,1)S(1)}, pred[2]{0:T(512)(128)(4,1)}, u32[]{:S(2)}) copy-start(pred[2]{0:T(512)(128)(4,1)} %get-tuple-element.269) | copy-start | bytes 10
  122.3 41.4 %copy-start.94 = (pred[2]{0:T(512)(128)(4,1)S(1)}, pred[2]{0:T(512)(128)(4,1)}, u32[]{:S(2)}) copy-start(pred[2]{0:T(512)(128)(4,1)} %get-tuple-element.270) | copy-start | bytes 10
  122.3 44.9 %copy-start.93 = (pred[2]{0:T(512)(128)(4,1)S(1)}, pred[2]{0:T(512)(128)(4,1)}, u32[]{:S(2)}) copy-start(pred[2]{0:T(512)(128)(4,1)} %get-tuple-element.271) | copy-start | bytes 10
  122.3 47.8 %copy-start.92 = (pred[2]{0:T(512)(128)(4,1)S(1)}, pred[2]{0:T(512)(128)(4,1)}, u32[]{:S(2)}) copy-start(pred[2]{0:T(512)(128)(4,1)} %get-tuple-element.272) | copy-start | bytes 10
  122.4 51.2 %copy-start.116 = (pred[2]{0:T(512)(128)(4,1)S(1)}, pred[2]{0:T(512)(128)(4,1)}, u32[]{:S(2)}) copy-start(pred[2]{0:T(512)(128)(4,1)} %compare_and_fusion.26) | copy-start | bytes 10
  122.4 51.4 %copy-start.76 = (bf16[2,8,256]{2,1,0:T(8,128)(2,1)S(1)}, bf16[2,8,256]{2,1,0:T(8,128)(2,1)}, u32[]{:S(2)}) copy-start(bf16[2,8,256]{2,1,0:T(8,128)(2,1)} %gather_fusion.44) | copy-start | bytes 24580
  122.4 51.4 %copy-start.77 = (bf16[2,8,256]{2,1,0:T(8,128)(2,1)S(1)}, bf16[2,8,256]{2,1,0:T(8,128)(2,1)}, u32[]{:S(2)}) copy-start(bf16[2,8,256]{2,1,0:T(8,128)(2,1)} %gather_fusion.17) | copy-start | bytes 24580
  122.4 51.4 %copy-start.110 = (pred[2]{0:T(512)(128)(4,1)S(1)}, pred[2]{0:T(512)(128)(4,1)}, u32[]{:S(2)}) copy-start(pred[2]{0:T(512)(128)(4,1)} %get-tuple-element.224) | copy-start | bytes 10
  122.4 51.5 %copy-start.113 = (pred[2]{0:T(512)(128)(4,1)S(1)}, pred[2]{0:T(512)(128)(4,1)}, u32[]{:S(2)}) copy-start(pred[2]{0:T(512)(128)(4,1)} %get-tuple-element.225) | copy-start | bytes 10
  122.4 51.6 %copy-start.78 = (bf16[2,8,256]{2,1,0:T(8,128)(2,1)S(1)}, bf16[2,8,256]{2,1,0:T(8,128)(2,1)}, u32[]{:S(2)}) copy-start(bf16[2,8,256]{2,1,0:T(8,128)(2,1)} %gather_fusion.42) | copy-start | bytes 24580
  122.4 51.6 %copy-start.79 = (bf16[2,8,256]{2,1,0:T(8,128)(2,1)S(1)}, bf16[2,8,256]{2,1,0:T(8,128)(2,1)}, u32[]{:S(2)}) copy-start(bf16[2,8,256]{2,1,0:T(8,128)(2,1)} %gather_fusion.15) | copy-start | bytes 24580
  122.4 51.6 %copy-start.111 = (pred[2]{0:T(512)(128)(4,1)S(1)}, pred[2]{0:T(512)(128)(4,1)}, u32[]{:S(2)}) copy-start(pred[2]{0:T(512)(128)(4,1)} %get-tuple-element.226) | copy-start | bytes 10
  122.4 51.8 %copy-start.109 = (pred[2]{0:T(512)(128)(4,1)S(1)}, pred[2]{0:T(512)(128)(4,1)}, u32[]{:S(2)}) copy-start(pred[2]{0:T(512)(128)(4,1)} %get-tuple-element.227) | copy-start | bytes 10
  122.4 52.1 %copy-start.122 = (pred[2]{0:T(512)(128)(4,1)S(1)}, pred[2]{0:T(512)(128)(4,1)}, u32[]{:S(2)}) copy-start(pred[2]{0:T(512)(128)(4,1)} %compare_and_fusion.13) | copy-start | bytes 10
  137.0 48.5 %copy-start.9 = (bf16[2,8,8,1,256]{4,3,2,1,0:T(2,128)(2,1)}, bf16[2,8,8,1,256]{4,3,2,1,0:T(2,128)(2,1)S(1)}, u32[]{:S(2)}) copy-start(bf16[2,8,8,1,256]{4,3,2,1,0:T(2,128)(2,1)S(1)} %broadcast_select_fusion.2) | copy-start | bytes 196612
  137.9 38.7 %copy-start.11 = (bf16[2,8,8,1,256]{4,3,2,1,0:T(2,128)(2,1)}, bf16[2,8,8,1,256]{4,3,2,1,0:T(2,128)(2,1)S(1)}, u32[]{:S(2)}) copy-start(bf16[2,8,8,1,256]{4,3,2,1,0:T(2,128)(2,1)S(1)} %copy.561) | copy-start | bytes 196612
  146.6 37.2 %copy-start.43 = (bf16[2,8,1,1,256]{4,3,2,1,0:T(2,128)(2,1)}, bf16[2,8,1,1,256]{4,3,2,1,0:T(2,128)(2,1)S(1)}, u32[]{:S(2)}) copy-start(bf16[2,8,1,1,256]{4,3,2,1,0:T(2,128)(2,1)S(1)} %broadcast_select_fusion.8) | copy-start | bytes 24580
  183.8 9.8 %copy-start.18 = (bf16[2,8,8,8,256]{4,3,2,1,0:T(8,128)(2,1)}, bf16[2,8,8,8,256]{4,3,2,1,0:T(8,128)(2,1)S(1)}, u32[]{:S(2)}) copy-start(bf16[2,8,8,8,256]{4,3,2,1,0:T(8,128)(2,1)S(1)} %get-tuple-element.164) | copy-start | bytes 1572868
  183.8 10.5 %copy-start.16 = (bf16[2,8,8,8,256]{4,3,2,1,0:T(8,128)(2,1)}, bf16[2,8,8,8,256]{4,3,2,1,0:T(8,128)(2,1)S(1)}, u32[]{:S(2)}) copy-start(bf16[2,8,8,8,256]{4,3,2,1,0:T(8,128)(2,1)S(1)} %get-tuple-element.163) | copy-start | bytes 1572868
  183.8 4.9 %copy-start.28 = (bf16[2,8,8,8,256]{4,0,3,2,1:T(2,128)(2,1)S(1)}, bf16[2,8,8,8,256]{4,0,3,2,1:T(2,128)(2,1)}, u32[]{:S(2)}) copy-start(bf16[2,8,8,8,256]{4,0,3,2,1:T(2,128)(2,1)} %copy-done.27) | copy-start | bytes 1572868
  185.6 7.5 %copy-start.5 = (bf16[2,8,9,10,256]{4,3,2,1,0:T(8,128)(2,1)}, bf16[2,8,9,10,256]{4,3,2,1,0:T(8,128)(2,1)S(1)}, u32[]{:S(2)}) copy-start(bf16[2,8,9,10,256]{4,3,2,1,0:T(8,128)(2,1)S(1)} %get-tuple-element.160) | copy-start | bytes 2211844
  185.6 9.8 %copy-start.3 = (bf16[2,8,9,10,256]{4,3,2,1,0:T(8,128)(2,1)}, bf16[2,8,9,10,256]{4,3,2,1,0:T(8,128)(2,1)S(1)}, u32[]{:S(2)}) copy-start(bf16[2,8,9,10,256]{4,3,2,1,0:T(8,128)(2,1)S(1)} %get-tuple-element.159) | copy-start | bytes 2211844
  195.6 3.3 copy-start.48
  195.6 3.3 copy-start.49
  195.6 3.3 copy-start.115
  195.6 4.0 %copy-start.74 = (bf16[2,8,256]{2,1,0:T(8,128)(2,1)S(1)}, bf16[2,8,256]{2,1,0:T(8,128)(2,1)}, u32[]{:S(2)}) copy-start(bf16[2,8,256]{2,1,0:T(8,128)(2,1)} %gather_fusion.48) | copy-start | bytes 24580
  195.6 4.0 %copy-start.75 = (bf16[2,8,256]{2,1,0:T(8,128)(2,1)S(1)}, bf16[2,8,256]{2,1,0:T(8,128)(2,1)}, u32[]{:S(2)}) copy-start(bf16[2,8,256]{2,1,0:T(8,128)(2,1)} %gather_fusion.21) | copy-start | bytes 24580
  195.6 4.0 %copy-start.114 = (pred[2]{0:T(512)(128)(4,1)S(1)}, pred[2]{0:T(512)(128)(4,1)}, u32[]{:S(2)}) copy-start(pred[2]{0:T(512)(128)(4,1)} %get-tuple-element.220) | copy-start | bytes 10
  195.6 4.7 %copy-start.103 = (bf16[2,256]{1,0:T(2,128)(2,1)S(1)}, bf16[2,256]{1,0:T(2,128)(2,1)}, u32[]{:S(2)}) copy-start(bf16[2,256]{1,0:T(2,128)(2,1)} %gather_fusion.47) | copy-start | bytes 3076
  195.6 4.7 %copy-start.105 = (bf16[2,256]{1,0:T(2,128)(2,1)S(1)}, bf16[2,256]{1,0:T(2,128)(2,1)}, u32[]{:S(2)}) copy-start(bf16[2,256]{1,0:T(2,128)(2,1)} %gather_fusion.20) | copy-start | bytes 3076
  195.7 4.7 %copy-start.121 = (pred[2]{0:T(512)(128)(4,1)S(1)}, pred[2]{0:T(512)(128)(4,1)}, u32[]{:S(2)}) copy-start(pred[2]{0:T(512)(128)(4,1)} %get-tuple-element.221) | copy-start | bytes 10
  195.7 5.3 %copy-start.82 = (bf16[2,8,256]{2,1,0:T(8,128)(2,1)S(1)}, bf16[2,8,256]{2,1,0:T(8,128)(2,1)}, u32[]{:S(2)}) copy-start(bf16[2,8,256]{2,1,0:T(8,128)(2,1)} %gather_fusion.46) | copy-start | bytes 24580
  195.7 5.3 %copy-start.83 = (bf16[2,8,256]{2,1,0:T(8,128)(2,1)S(1)}, bf16[2,8,256]{2,1,0:T(8,128)(2,1)}, u32[]{:S(2)}) copy-start(bf16[2,8,256]{2,1,0:T(8,128)(2,1)} %gather_fusion.19) | copy-start | bytes 24580
  195.7 5.3 %copy-start.112 = (pred[2]{0:T(512)(128)(4,1)S(1)}, pred[2]{0:T(512)(128)(4,1)}, u32[]{:S(2)}) copy-start(pred[2]{0:T(512)(128)(4,1)} %get-tuple-element.222) | copy-start | bytes 10
  195.7 5.9 %copy-start.104 = (bf16[2,256]{1,0:T(2,128)(2,1)S(1)}, bf16[2,256]{1,0:T(2,128)(2,1)}, u32[]{:S(2)}) copy-start(bf16[2,256]{1,0:T(2,128)(2,1)} %gather_fusion.45) | copy-start | bytes 3076
  195.7 5.9 %copy-start.106 = (bf16[2,256]{1,0:T(2,128)(2,1)S(1)}, bf16[2,256]{1,0:T(2,128)(2,1)}, u32[]{:S(2)}) copy-start(bf16[2,256]{1,0:T(2,128)(2,1)} %gather_fusion.18) | copy-start | bytes 3076
  195.7 5.9 %copy-start.118 = (pred[2]{0:T(512)(128)(4,1)S(1)}, pred[2]{0:T(512)(128)(4,1)}, u32[]{:S(2)}) copy-start(pred[2]{0:T(512)(128)(4,1)} %get-tuple-element.223) | copy-start | bytes 10
  195.7 6.6 %copy-start.10 = (bf16[2,8,8,1,256]{4,3,2,1,0:T(2,128)(2,1)S(1)}, bf16[2,8,8,1,256]{4,3,2,1,0:T(2,128)(2,1)}, u32[]{:S(2)}) copy-start(bf16[2,8,8,1,256]{4,3,2,1,0:T(2,128)(2,1)} %copy-done.9) | copy-start | bytes 196612
  195.7 6.6 %copy-start.44 = (bf16[2,8,1,1,256]{4,3,2,1,0:T(2,128)(2,1)S(1)}, bf16[2,8,1,1,256]{4,3,2,1,0:T(2,128)(2,1)}, u32[]{:S(2)}) copy-start(bf16[2,8,1,1,256]{4,3,2,1,0:T(2,128)(2,1)} %copy-done.43) | copy-start | bytes 24580
  223.4 167.0 %reduce-scatter.5.cloned.1.call-start = ((), (), s32[]{:S(2)}) async-start(), calls=%async_computation.3 | async-start | bytes 4718592 | tf_op jit(solution)/shard_map/reduce_scatter | solution.py:146
  223.4 3.1 copy-start.2
  (65 other events, 101.2 us)
Sparse Core Ops, SparseCore 0:
  223.5 72.7 reduce-scatter.2
  302.2 88.1 reduce-scatter.4
where the time goes:
time: 407 us; the launch traced here: 400 us
  local copies, waits for them, and re-layouts  132 us (32%)
  waiting for transfers between devices  129 us (32%)
  other arithmetic  69.9 us (17%)
  matrix products  38.9 us (10%)
  between operations  17.5 us (4%)
  starting transfers between devices  12.2 us (3%)
    reduce_scatter x1, waiting for transfers between devices, per_device(): lax.psum_scatter(across_scene, 'space', scatter_dimension=1, tiled=True)  73 us
    gather x54, local copies, waits for them, and re-layouts, assemble(): blocks.append(jnp.take(corner, lookup[:, column], axis=0))  67.3 us
    reduce_scatter x1, waiting for transfers between devices, per_device(): lax.psum_scatter(grad_terms, 'scene', scatter_dimension=2, tiled=True)  41.8 us
    another operation x43, local copies, waits for them, and re-layouts, assemble(): blocks.append(jnp.take(corner, lookup[:, column], axis=0))  25.9 us
    select_n x58, other arithmetic, assemble(): blocks.append(jnp.take(corner, lookup[:, column], axis=0))  17.7 us
    dot_general x27, matrix products, forward_conv(): jnp.dot(window_rows(padded, offset_xyz, extent), weight[column], preferre...  17.1 us
    ppermute x2, waiting for transfers between devices, extended(): lax.ppermute(tail, axis, [(i, (i + 1) % count) for i in range(ends)])  14.3 us
    gather x23, other arithmetic  13.7 us
  transfers between devices with their start and end apart: 6, of which 4 were waited for; matrix products, arithmetic and copies ran while one was open for 16% of the time, Pallas kernels for 0%

commit v1 on v0

v1 whole, which is shorter than its diff:
```python
import functools

import jax
import jax.numpy as jnp
from jax import lax
from jax.experimental import pallas as pl
from jax.experimental.pallas import tpu as pltpu
from jax.sharding import PartitionSpec as P

MESH = pl.DeviceIdType.MESH
VMEM_BYTES = 56 * 1024 * 1024
GROUP = 3


def both_sides(cells):
    count = lax.axis_size("space")
    ends = count - 1
    left = lax.ppermute(cells, "space", [(i, i + 1) for i in range(ends)])
    right = lax.ppermute(cells, "space", [(i + 1, i) for i in range(ends)])
    return left, right


def spans(shift):
    if shift < 0:
        return slice(7, 8), slice(0, 1)
    if shift == 0:
        return slice(0, 8), slice(1, 9)
    return slice(0, 1), slice(9, 10)


def spans_z(shift):
    if shift < 0:
        return slice(7, 8), slice(7, 8)
    if shift == 0:
        return slice(0, 8), slice(8, 16)
    return slice(0, 1), slice(16, 17)


def fill_copies(lookup, bricks, sides, window, staged, copies):
    channels = staged.shape[-1]
    for side, ref in enumerate(sides):
        for b in range(bricks):

            def widen(x, carry, ref=ref, b=b, at=side * bricks + b):
                rows = ref[b, pl.ds(pl.multiple_of(x * 64, 64), 64), :]
                window[at, x] = rows.astype(jnp.float32).reshape(8, 8, channels)
                return carry

            lax.fori_loop(0, 8, widen, 0)
    for b in range(bricks):
        for sx in (-1, 0, 1):
            for sy in (-1, 0, 1):
                for sz in (-1, 0, 1):
                    (from_x, to_x), (from_y, to_y), (from_z, to_z) = spans(sx), spans(sy), spans_z(sz)
                    if sx == sy == sz == 0:
                        staged[to_x, to_y, to_z, :] = window[bricks + b, from_x, from_y, from_z, :]
                        continue
                    at = lookup[b, 9 * (sx + 1) + 3 * (sy + 1) + sz + 1]
                    inside = (at >= 0).astype(jnp.float32)
                    taken = window[jnp.maximum(at, 0), from_x, from_y, from_z, :]
                    staged[to_x, to_y, to_z, :] = taken * inside
        for y in range(3):
            for z in range(3):

                def pack(x, carry, b=b, y=y, z=z):
                    rows = staged[x, y : y + 8, 7 + z : 15 + z, :]
                    copies[y, b, pl.ds(pl.multiple_of(x * 64, 64), 64), z * channels : (z + 1) * channels] = (
                        rows.reshape(64, channels).astype(jnp.bfloat16)
                    )
                    return carry

                lax.fori_loop(0, 10, pack, 0)


def conv_kernel(
    lookup, features, active, hidden_t,
    hid_left, hidden, hid_right, grad_left, grad, grad_right, weight, weight_t,
    outputs, input_grad, terms,
    window, staged, hid_copies, grad_copies, total,
):
    bricks = hidden.shape[0]
    channels = hidden.shape[-1]

    def rows_of(copies, i, b):
        start = pl.multiple_of((i // 3) * 64, 64)
        return copies[i % 3, b, pl.ds(start, 512), :]

    fill_copies(lookup, bricks, (grad_left, grad, grad_right), window, staged, grad_copies)

    def gradient(i, carry):
        for z in range(3):
            summed = None
            for b in range(bricks):
                start = pl.multiple_of((i // 3) * 64, 64)
                rows = grad_copies[i % 3, b, pl.ds(start, 512), z * channels : (z + 1) * channels]
                product = jnp.dot(hidden_t[b], rows, preferred_element_type=jnp.float32)
                summed = product if summed is None else summed + product
            tap = 26 - 3 * i - z
            half = channels // 2
            terms[tap, 0] = summed[:, :half]
            terms[tap, 1] = summed[:, half:]
        return carry

    lax.fori_loop(0, 9, gradient, 0)
    fill_copies(lookup, bricks, (hid_left, hidden, hid_right), window, staged, hid_copies)

    for b in range(bricks):
        for copies, matrix in ((hid_copies, weight), (grad_copies, weight_t)):
            total[...] = jnp.zeros_like(total)

            def step(i, carry, b=b, copies=copies, matrix=matrix):
                total[...] += jnp.dot(rows_of(copies, i, b), matrix[i], preferred_element_type=jnp.float32)
                return carry

            lax.fori_loop(0, 9, step, 0)
            if copies is hid_copies:
                summed = (features[b].astype(jnp.float32) + total[...]) * active[b]
                outputs[b] = summed.astype(jnp.bfloat16)
            else:
                kept = jnp.where(hidden[b].astype(jnp.float32) > 0, total[...], 0.0)
                input_grad[b] = (grad[b].astype(jnp.float32) + kept).astype(jnp.bfloat16)


def convolve(lookup, features, active, hidden_t, hiddens, grads, weight, weight_t):
    bricks, voxels, channels = features.shape
    vmem = pl.BlockSpec(memory_space=pltpu.VMEM)
    return pl.pallas_call(
        conv_kernel,
        out_shape=(
            jax.ShapeDtypeStruct(features.shape, jnp.bfloat16),
            jax.ShapeDtypeStruct(features.shape, jnp.bfloat16),
            jax.ShapeDtypeStruct((27, 2, channels, channels // 2), jnp.float32),
        ),
        in_specs=[pl.BlockSpec(memory_space=pltpu.SMEM)] + [vmem] * 11,
        out_specs=(vmem, vmem, vmem),
        scratch_shapes=[
            pltpu.VMEM((3 * bricks, 8, 8, 8, channels), jnp.float32),
            pltpu.VMEM((10, 10, 24, channels), jnp.float32),
            pltpu.VMEM((3, bricks, 640, 3 * channels), jnp.bfloat16),
            pltpu.VMEM((3, bricks, 640, 3 * channels), jnp.bfloat16),
            pltpu.VMEM((voxels, channels), jnp.float32),
        ],
        compiler_params=pltpu.CompilerParams(vmem_limit_bytes=VMEM_BYTES),
    )(lookup, features, active, hidden_t, *hiddens, *grads, weight, weight_t)


def scatter_kernel(scale, terms, result, r0, r1, r2, r3, r4, r5, send, recv):
    space, scene = lax.axis_index("space"), lax.axis_index("scene")
    core, x = scene % 2, scene // 2
    y, low, high = space % 2, (space // 2) % 2, space // 4
    partner = {
        "core": (space, scene + 1 - 2 * core),
        "x": (space, scene + 2 - 4 * x),
        "y": (space + 1 - 2 * y, scene),
        "low": (space + 2 - 4 * low, scene),
        "high": (space + 4 - 8 * high, scene),
    }
    barrier = pltpu.get_barrier_semaphore()
    for device in partner.values():
        pl.semaphore_signal(barrier, inc=1, device_id=device, device_id_type=MESH)
    pl.semaphore_wait(barrier, 5)

    chunks = r0.shape[0]
    copies = {}

    def begin(stage, k, source, target, axis):
        copy = pltpu.make_async_remote_copy(
            src_ref=source, dst_ref=target, send_sem=send.at[stage, k], recv_sem=recv.at[stage, k],
            device_id=partner[axis], device_id_type=MESH,
        )
        copy.start()
        copies[stage, k] = copy

    def advance(stage, k):
        taps = pl.ds(GROUP * k, GROUP)
        x_first = k % 2 == 0
        if stage == 0:
            begin(0, k, terms.at[taps, :, :, :, :, 1 - core], r0.at[k], "core")
            return
        copies[stage - 1, k].wait_recv()
        if stage == 1:
            r0[k] = r0[k] + terms[taps, :, :, :, :, core]
            if x_first:
                begin(1, k, r0.at[k, :, 1 - x], r1.at[k], "x")
            else:
                begin(1, k, r0.at[k, :, :, :, :, 1 - y], r1.at[k], "y")
        elif stage == 2:
            if x_first:
                r1[k] = r1[k] + r0[k, :, x]
                begin(2, k, r1.at[k, :, :, :, 1 - y], r2.at[k], "y")
            else:
                r1[k] = r1[k] + r0[k, :, :, :, :, y]
                begin(2, k, r1.at[k, :, 1 - x], r2.at[k], "x")
        elif stage == 3:
            r2[k] = r2[k] + (r1[k, :, :, :, y] if x_first else r1[k, :, x])
            begin(3, k, r2.at[k, :, :, 1 - low], r3.at[k], "low")
        elif stage == 4:
            r3[k] = r3[k] + r2[k, :, :, low]
            begin(4, k, r3.at[k, :, 1 - high], r4.at[k], "high")
        elif stage == 5:
            r4[k] = r4[k] + r3[k, :, high]
            begin(5, k, r4.at[k], r5.at[k], "core")
        else:
            mine, other = r4[k] * scale, r5[k] * scale
            first = jnp.where(core == 0, mine, other)
            second = jnp.where(core == 0, other, mine)
            both = jnp.concatenate([first, second], axis=1)
            half = both.shape[-1] // 2
            result[taps] = jnp.where(core == 0, both[:, :, :half], both[:, :, half:])

    ahead = 2
    for k in range(min(ahead, chunks)):
        advance(0, k)
    for at in range(chunks + 6):
        if at + ahead < chunks:
            advance(0, at + ahead)
        for stage in range(1, 7):
            k = at - (stage - 1)
            if 0 <= k < chunks:
                advance(stage, k)
    for copy in copies.values():
        copy.wait_send()


def scatter_sum(terms, scale):
    taps, _, channels, half = terms.shape
    rows = channels // 16
    chunks = taps // GROUP
    vmem = pl.BlockSpec(memory_space=pltpu.VMEM)
    f32 = jnp.float32
    tail = (rows, half)
    return pl.pallas_call(
        functools.partial(scatter_kernel, scale),
        out_shape=jax.ShapeDtypeStruct((taps, 2 * rows, half // 2), f32),
        in_specs=[vmem],
        out_specs=vmem,
        scratch_shapes=[
            pltpu.VMEM((chunks, GROUP, 2, 2, 2, 2) + tail, f32),
            pltpu.VMEM((chunks, GROUP, 2, 2, 2) + tail, f32),
            pltpu.VMEM((chunks, GROUP, 2, 2) + tail, f32),
            pltpu.VMEM((chunks, GROUP, 2) + tail, f32),
            pltpu.VMEM((chunks, GROUP) + tail, f32),
            pltpu.VMEM((chunks, GROUP) + tail, f32),
            pltpu.SemaphoreType.DMA((6, chunks)),
            pltpu.SemaphoreType.DMA((6, chunks)),
        ],
        compiler_params=pltpu.CompilerParams(
            collective_id=0, has_side_effects=True, vmem_limit_bytes=VMEM_BYTES
        ),
    )(terms.reshape(taps, 2, 2, 2, 2, 2, rows, half))


def per_device(features, cotangent, weight, counts, neighbours, occupancy):
    shape = features.shape
    bricks, extent, channels = shape[1], shape[2], shape[-1]
    voxels = extent * extent * extent
    feats = features.reshape(bricks, voxels, channels)
    slot_live = (jnp.arange(bricks, dtype=jnp.int32) < counts[0, 0]).astype(jnp.int32)
    active = (occupancy[0] * slot_live[:, None]).reshape(bricks, voxels, 1)
    live = active.astype(jnp.bfloat16)
    grad = cotangent.reshape(bricks, voxels, channels) * live
    hidden = jnp.maximum(feats, 0) * live
    grad_left, grad_right = both_sides(grad)
    hid_left, hid_right = both_sides(hidden)
    first_id = (lax.axis_index("space") - 1) * bricks
    linked = neighbours[0]
    local_ids = jnp.where(linked >= 0, linked - first_id, -1)
    centre = (bricks + jnp.arange(bricks, dtype=jnp.int32))[:, None]
    lookup = jnp.concatenate([local_ids[:, :13], centre, local_ids[:, 13:]], axis=1)
    weight_t = weight[::-1].swapaxes(1, 2).reshape(9, 3 * channels, channels)
    outputs, input_grad, terms = convolve(
        lookup, feats, active.astype(jnp.float32), hidden.swapaxes(1, 2),
        (hid_left, hidden, hid_right), (grad_left, grad, grad_right),
        weight.reshape(9, 3 * channels, channels), weight_t,
    )
    space, scene = lax.axis_size("space"), lax.axis_size("scene")
    scale = float(scene * space * bricks * voxels) ** (-0.5)
    if (space, scene) == (8, 4):
        weight_grad = scatter_sum(terms, scale)
    else:
        whole = jnp.concatenate([terms[:, 0], terms[:, 1]], axis=2) * scale
        across = lax.psum_scatter(whole, "scene", scatter_dimension=2, tiled=True)
        weight_grad = lax.psum_scatter(across, "space", scatter_dimension=1, tiled=True)
    return outputs.reshape(shape), input_grad.reshape(shape), weight_grad


def solution(mesh):
    field = P("scene", "space", None, None, None, None)
    in_specs = (field, field, P(), P("scene", "space"), P("scene", "space", None), P("scene", "space", None))
    out_specs = (field, field, P(None, "space", "scene"))
    return jax.shard_map(per_device, mesh=mesh, in_specs=in_specs, out_specs=out_specs, check_vma=False)
```

time: 407 us -> 147 us (0.36); the launches traced: 400 us -> 146 us
  local copies, waits for them, and re-layouts: 132 us -> 10.8 us
  waiting for transfers between devices: 129 us -> 25.3 us
  Pallas kernels: 0 us -> 89.6 us
  other arithmetic: 69.9 us -> 6.4 us
  matrix products: 38.9 us -> 0 us
  between operations: 17.5 us -> 1.33 us
    reduce_scatter x2 -> x0, waiting for transfers between devices: 115 us -> none  [the longest x1 73 us: per_device(): lax.psum_scatter(across_scene, 'space', scatter_dimension=1, tiled=True)]
    pallas_call x0 -> x2, Pallas kernels: none -> 89.6 us  [the longest x1 57 us: scatter_sum(): pl.pallas_call(functools.partial(scatter_kernel, scale), out_shape=jax.Sh...]
    gather x54 -> x0, local copies, waits for them, and re-layouts: 67.3 us -> none  [assemble(): blocks.append(jnp.take(corner, lookup[:, column], axis=0))]
    dot_general x81 -> x0, matrix products: 38.9 us -> none  [the longest x27 17.1 us: forward_conv(): jnp.dot(window_rows(padded, offset_xyz, extent), weight[column], preferre...]
    another operation x43 -> x0, local copies, waits for them, and re-layouts: 25.9 us -> none  [assemble(): blocks.append(jnp.take(corner, lookup[:, column], axis=0))]
    concatenate x12 -> x1, other arithmetic: 19.4 us -> 0.64 us  [per_device(): jnp.concatenate([local_ids[:, :13], centre, local_ids[:, 13:]], axis=1)]
    select_n x59 -> x1, other arithmetic: 18.4 us -> 0.68 us  [per_device(): local_ids = jnp.where(linked >= 0, linked - first_id, -1)]
    gather x23 -> x0, other arithmetic: 13.7 us -> none
  transfers between devices with their start and end apart: 6 -> 4, of which waited for: 4 -> 2; matrix products, arithmetic and copies ran while one was open for 16% -> 8% of each run, Pallas kernels for 0% -> 0%
where the time goes in v1:
time: 147 us; the launch traced here: 146 us
  Pallas kernels  89.6 us (61%)
  waiting for transfers between devices  25.3 us (17%)
  starting transfers between devices  12.9 us (9%)
  local copies, waits for them, and re-layouts  10.8 us (7%)
  other arithmetic  6.4 us (4%)
    pallas_call x1, Pallas kernels, scatter_sum(): pl.pallas_call(functools.partial(scatter_kernel, scale), out_shape=jax.Sh...  57 us
    pallas_call x1, Pallas kernels, convolve(): pl.pallas_call(conv_kernel, out_shape=(jax.ShapeDtypeStruct(features.shap...  32.5 us
    ppermute x2, waiting for transfers between devices, both_sides(): left = lax.ppermute(cells, 'space', [(i, i + 1) for i in range(ends)])  25.3 us
    ppermute x2, starting transfers between devices, both_sides(): left = lax.ppermute(cells, 'space', [(i, i + 1) for i in range(ends)])  10.4 us
    transpose x2, local copies, waits for them, and re-layouts, per_device(): weight_t = weight[::-1].swapaxes(1, 2).reshape(9, 3 * channels, channels)  5.87 us
  transfers between devices with their start and end apart: 4, of which 2 were waited for; matrix products, arithmetic and copies ran while one was open for 8% of the time, Pallas kernels for 0%

profile of v1, /device:TPU:1, one launch (start us, length us, event | category | flops | bytes accessed | tf_op | source)
XLA Modules:
  0.0 146.3 jit_solution(11840347827999387069)
XLA Ops:
  1.3 0.8 fusion
  2.0 2.4 %broadcast_multiply_fusion = (bf16[2,512,256]{2,1,0:T(8,128)(2,1)}, bf16[2,512,256]{2,1,0:T(8,128)(2,1)}) fusion(bf16[2,512,256]{2,1,0:T(8,128)(2,1)} %bitcast.24, bf16[2,512]{1,0:T(2,128)(2,1)S(1)} %fusion, bf16[2,512,256]{2,1,0:T(8,128)(2,1)} %bitcast.22), kind=kLoop, calls=%fused_computation.3 | loop fusion | flops 786432 | bytes 2099200 | tf_op jit(solution)/shard_map/mul | solution.py:261
  4.4 1.3 collective-permute-start.3
  5.7 5.4 %collective-permute-start.2 = (bf16[2,512,256]{2,1,0:T(8,128)(2,1)}, bf16[2,512,256]{2,1,0:T(8,128)(2,1)}, u32[]{:S(2)}, u32[]{:S(2)}) collective-permute-start(bf16[2,512,256]{2,1,0:T(8,128)(2,1)} %get-tuple-element.9.grad), channel_id=1, source_target_pairs={{0,4},{4,8},{8,12},{12,16},{16,20},{20,24},{24,28},{1,5},{5,9},{9,... | collective-permute-start | bytes 1572872 | tf_op jit(solution)/shard_map/ppermute | solution.py:18
  11.1 1.3 collective-permute-start.1
  12.4 4.9 %collective-permute-start = (bf16[2,512,256]{2,1,0:T(8,128)(2,1)}, bf16[2,512,256]{2,1,0:T(8,128)(2,1)}, u32[]{:S(2)}, u32[]{:S(2)}) collective-permute-start(bf16[2,512,256]{2,1,0:T(8,128)(2,1)} %get-tuple-element.10.hidden), channel_id=1, source_target_pairs={{0,4},{4,8},{8,12},{12,16},{16,20},{20,24},{24,28},{1,5},{5,9},{9,... | collective-permute-start | bytes 1572872 | tf_op jit(solution)/shard_map/ppermute | solution.py:18
  17.3 0.7 fusion.1
  18.0 0.1 fusion.2
  18.1 0.0 copy-start
  18.1 2.2 %reverse_bitcast_fusion = bf16[27,256,256]{1,2,0:T(8,128)(2,1)S(1)} fusion(bf16[27,256,256]{2,1,0:T(8,128)(2,1)} %param.8), kind=kLoop, calls=%fused_computation | loop fusion | bytes 7077888 | tf_op jit(solution)/shard_map/transpose | solution.py:270
  20.4 0.0 copy-done
  20.4 1.0 copy.14
  21.4 2.0 %copy.17.hidden_t = bf16[2,256,512]{2,1,0:T(8,128)(2,1)} copy(bf16[2,256,512]{1,2,0:T(8,128)(2,1)} %bitcast.5) | data formatting | bytes 1048576 | tf_op jit(solution)/shard_map/transpose | solution.py:272
  23.4 3.6 %copy.16 = bf16[27,256,256]{2,1,0:T(8,128)(2,1)} copy(bf16[27,256,256]{1,2,0:T(8,128)(2,1)S(1)} %reverse_bitcast_fusion) | data formatting | bytes 7077888 | tf_op jit(solution)/shard_map/transpose | solution.py:270
  27.1 0.6 pad_add_fusion.lookup
  27.7 1.9 %multiply_convert_fusion.active = f32[2,512,1]{2,1,0:T(8,128)} fusion(s32[2,512,1]{2,1,0:T(8,128)} %copy.14, s32[2]{0:T(128)S(1)} %compare_convert_fusion), kind=kLoop, calls=%fused_computation.2 | loop fusion | flops 2048 | bytes 8200 | tf_op jit(solution)/shard_map/convert_element_type | solution.py:272
  29.6 0.0 collective-permute-done.3.grad_right
  29.6 14.1 %collective-permute-done.2.grad_left = bf16[2,512,256]{2,1,0:T(8,128)(2,1)} collective-permute-done((bf16[2,512,256]{2,1,0:T(8,128)(2,1)}, bf16[2,512,256]{2,1,0:T(8,128)(2,1)}, u32[]{:S(2)}, u32[]{:S(2)}) %collective-permute-start.2) | collective-permute-done | bytes 524320 | tf_op jit(solution)/shard_map/ppermute | solution.py:18
  43.7 0.0 collective-permute-done.1.hid_right
  43.7 11.2 %collective-permute-done.hid_left = bf16[2,512,256]{2,1,0:T(8,128)(2,1)} collective-permute-done((bf16[2,512,256]{2,1,0:T(8,128)(2,1)}, bf16[2,512,256]{2,1,0:T(8,128)(2,1)}, u32[]{:S(2)}, u32[]{:S(2)}) %collective-permute-start) | collective-permute-done | bytes 524320 | tf_op jit(solution)/shard_map/ppermute | solution.py:18
  54.9 32.5 %shard_map.85 = (bf16[2,512,256]{2,1,0:T(8,128)(2,1)}, bf16[2,512,256]{2,1,0:T(8,128)(2,1)}, f32[27,2,256,128]{3,2,1,0:T(8,128)}) custom-call(s32[2,27]{1,0:T(2,128)} %pad_add_fusion.lookup, bf16[2,512,256]{2,1,0:T(8,128)(2,1)} %bitcast.23, f32[2,512,1]{2,1,0:T(8,128)} %multiply_convert_fusion.active, bf16[2,256,512]{2,1,0:T(8,128)(2,1)} %copy.17.hidden_t, ...), custom_call_target="tpu_custom_call" | custom-call | tf_op jit(solution)/shard_map/pallas_call | solution.py:127
  87.5 57.0 %shard_map.86 = f32[27,32,64]{2,1,0:T(8,128)} custom-call(f32[27,2,2,2,2,2,16,128]{7,6,5,4,3,2,1,0:T(8,128)} %bitcast.21), custom_call_target="tpu_custom_call" | custom-call | tf_op jit(solution)/shard_map/pallas_call | solution.py:232
  144.5 1.8 %copy.20 = f32[27,32,64]{2,1,0:T(8,128)} copy(f32[27,32,64]{2,1,0:T(8,128)} %shard_map.86) | data formatting | bytes 442368
  (2 shorter events, 0.0 us)
Async XLA Ops:
  4.4 25.2 %collective-permute-start.3 = (bf16[2,512,256]{2,1,0:T(8,128)(2,1)}, bf16[2,512,256]{2,1,0:T(8,128)(2,1)}, u32[]{:S(2)}, u32[]{:S(2)}) collective-permute-start(bf16[2,512,256]{2,1,0:T(8,128)(2,1)} %get-tuple-element.9.grad), channel_id=1, source_target_pairs={{4,0},{8,4},{12,8},{16,12},{20,16},{24,20},{28,24},{5,1},{9,5},{13... | collective-permute-start | bytes 1572872 | tf_op jit(solution)/shard_map/ppermute | solution.py:19
  5.7 38.0 %collective-permute-start.2 = (bf16[2,512,256]{2,1,0:T(8,128)(2,1)}, bf16[2,512,256]{2,1,0:T(8,128)(2,1)}, u32[]{:S(2)}, u32[]{:S(2)}) collective-permute-start(bf16[2,512,256]{2,1,0:T(8,128)(2,1)} %get-tuple-element.9.grad), channel_id=1, source_target_pairs={{0,4},{4,8},{8,12},{12,16},{16,20},{20,24},{24,28},{1,5},{5,9},{9,... | collective-permute-start | bytes 1572872 | tf_op jit(solution)/shard_map/ppermute | solution.py:18
  11.1 32.6 %collective-permute-start.1 = (bf16[2,512,256]{2,1,0:T(8,128)(2,1)}, bf16[2,512,256]{2,1,0:T(8,128)(2,1)}, u32[]{:S(2)}, u32[]{:S(2)}) collective-permute-start(bf16[2,512,256]{2,1,0:T(8,128)(2,1)} %get-tuple-element.10.hidden), channel_id=1, source_target_pairs={{4,0},{8,4},{12,8},{16,12},{20,16},{24,20},{28,24},{5,1},{9,5},{13... | collective-permute-start | bytes 1572872 | tf_op jit(solution)/shard_map/ppermute | solution.py:19
  12.4 42.5 %collective-permute-start = (bf16[2,512,256]{2,1,0:T(8,128)(2,1)}, bf16[2,512,256]{2,1,0:T(8,128)(2,1)}, u32[]{:S(2)}, u32[]{:S(2)}) collective-permute-start(bf16[2,512,256]{2,1,0:T(8,128)(2,1)} %get-tuple-element.10.hidden), channel_id=1, source_target_pairs={{0,4},{4,8},{8,12},{12,16},{16,20},{20,24},{24,28},{1,5},{5,9},{9,... | collective-permute-start | bytes 1572872 | tf_op jit(solution)/shard_map/ppermute | solution.py:18
  18.1 2.2 %copy-start = (s32[1,2,512]{2,1,0:T(2,128)S(1)}, s32[1,2,512]{2,1,0:T(2,128)}, u32[]{:S(2)}) copy-start(s32[1,2,512]{2,1,0:T(2,128)} %param.11) | copy-start | bytes 12292

commit v2 on v1

--- a/solution.py
+++ b/solution.py
@@ -10,6 +10,7 @@
 MESH = pl.DeviceIdType.MESH
 VMEM_BYTES = 56 * 1024 * 1024
 GROUP = 3
+LAG = 2
 
 
 def both_sides(cells):
@@ -72,79 +73,80 @@
                 lax.fori_loop(0, 10, pack, 0)
 
 
-def conv_kernel(
-    lookup, features, active, hidden_t,
-    hid_left, hidden, hid_right, grad_left, grad, grad_right, weight, weight_t,
-    outputs, input_grad, terms,
-    window, staged, hid_copies, grad_copies, total,
-):
-    bricks = hidden.shape[0]
-    channels = hidden.shape[-1]
-
-    def rows_of(copies, i, b):
-        start = pl.multiple_of((i // 3) * 64, 64)
-        return copies[i % 3, b, pl.ds(start, 512), :]
-
-    fill_copies(lookup, bricks, (grad_left, grad, grad_right), window, staged, grad_copies)
+def gradient_kernel(lookup, hidden_t, left, grad, right, terms, copies, window, staged):
+    bricks = grad.shape[0]
+    channels = grad.shape[-1]
+    half = channels // 2
+    fill_copies(lookup, bricks, (left, grad, right), window, staged, copies)
 
     def gradient(i, carry):
         for z in range(3):
             summed = None
             for b in range(bricks):
                 start = pl.multiple_of((i // 3) * 64, 64)
-                rows = grad_copies[i % 3, b, pl.ds(start, 512), z * channels : (z + 1) * channels]
+                rows = copies[i % 3, b, pl.ds(start, 512), z * channels : (z + 1) * channels]
                 product = jnp.dot(hidden_t[b], rows, preferred_element_type=jnp.float32)
                 summed = product if summed is None else summed + product
             tap = 26 - 3 * i - z
-            half = channels // 2
             terms[tap, 0] = summed[:, :half]
             terms[tap, 1] = summed[:, half:]
         return carry
 
     lax.fori_loop(0, 9, gradient, 0)
-    fill_copies(lookup, bricks, (hid_left, hidden, hid_right), window, staged, hid_copies)
-
-    for b in range(bricks):
-        for copies, matrix in ((hid_copies, weight), (grad_copies, weight_t)):
-            total[...] = jnp.zeros_like(total)
-
-            def step(i, carry, b=b, copies=copies, matrix=matrix):
-                total[...] += jnp.dot(rows_of(copies, i, b), matrix[i], preferred_element_type=jnp.float32)
-                return carry
-
-            lax.fori_loop(0, 9, step, 0)
-            if copies is hid_copies:
-                summed = (features[b].astype(jnp.float32) + total[...]) * active[b]
-                outputs[b] = summed.astype(jnp.bfloat16)
-            else:
-                kept = jnp.where(hidden[b].astype(jnp.float32) > 0, total[...], 0.0)
-                input_grad[b] = (grad[b].astype(jnp.float32) + kept).astype(jnp.bfloat16)
-
-
-def convolve(lookup, features, active, hidden_t, hiddens, grads, weight, weight_t):
-    bricks, voxels, channels = features.shape
-    vmem = pl.BlockSpec(memory_space=pltpu.VMEM)
+
+
+def blocks_kernel(lookup, left, hidden, right, copies, window, staged):
+    fill_copies(lookup, hidden.shape[0], (left, hidden, right), window, staged, copies)
+
+
+def vmem_specs(count):
+    return [pl.BlockSpec(memory_space=pltpu.VMEM)] * count
+
+
+def block_scratch(bricks, channels):
+    return [
+        pltpu.VMEM((3 * bricks, 8, 8, 8, channels), jnp.float32),
+        pltpu.VMEM((10, 10, 24, channels), jnp.float32),
+    ]
+
+
+def gradient_terms(lookup, hidden_t, grads):
+    bricks, voxels, channels = grads[1].shape
     return pl.pallas_call(
-        conv_kernel,
+        gradient_kernel,
         out_shape=(
-            jax.ShapeDtypeStruct(features.shape, jnp.bfloat16),
-            jax.ShapeDtypeStruct(features.shape, jnp.bfloat16),
             jax.ShapeDtypeStruct((27, 2, channels, channels // 2), jnp.float32),
+            jax.ShapeDtypeStruct((3, bricks, 640, 3 * channels), jnp.bfloat16),
         ),
-        in_specs=[pl.BlockSpec(memory_space=pltpu.SMEM)] + [vmem] * 11,
-        out_specs=(vmem, vmem, vmem),
-        scratch_shapes=[
-            pltpu.VMEM((3 * bricks, 8, 8, 8, channels), jnp.float32),
-            pltpu.VMEM((10, 10, 24, channels), jnp.float32),
-            pltpu.VMEM((3, bricks, 640, 3 * channels), jnp.bfloat16),
-            pltpu.VMEM((3, bricks, 640, 3 * channels), jnp.bfloat16),
-            pltpu.VMEM((voxels, channels), jnp.float32),
-        ],
+        in_specs=[pl.BlockSpec(memory_space=pltpu.SMEM)] + vmem_specs(4),
+        out_specs=tuple(vmem_specs(2)),
+        scratch_shapes=block_scratch(bricks, channels),
         compiler_params=pltpu.CompilerParams(vmem_limit_bytes=VMEM_BYTES),
-    )(lookup, features, active, hidden_t, *hiddens, *grads, weight, weight_t)
-
-
-def scatter_kernel(scale, terms, result, r0, r1, r2, r3, r4, r5, send, recv):
+        cost_estimate=pl.CostEstimate(
+            flops=2 * 27 * bricks * voxels * channels * channels, bytes_accessed=60_000_000, transcendentals=0
+        ),
+    )(lookup, hidden_t, *grads)
+
+
+def halo_blocks(lookup, hiddens):
+    bricks, voxels, channels = hiddens[1].shape
+    return pl.pallas_call(
+        blocks_kernel,
+        out_shape=jax.ShapeDtypeStruct((3, bricks, 640, 3 * channels), jnp.bfloat16),
+        in_specs=[pl.BlockSpec(memory_space=pltpu.SMEM)] + vmem_specs(3),
+        out_specs=vmem_specs(1)[0],
+        scratch_shapes=block_scratch(bricks, channels),
+        compiler_params=pltpu.CompilerParams(vmem_limit_bytes=VMEM_BYTES),
+        cost_estimate=pl.CostEstimate(flops=0, bytes_accessed=30_000_000, transcendentals=0),
+    )(lookup, *hiddens)
+
+
+def scatter_kernel(
+    scale, terms, features, active, hidden, grad, hid_source, weight_source, grad_source, weight_t_source,
+    outputs, input_grad, result,
+    hid_copies, weight, grad_copies, weight_t, total,
+    r0, r1, r2, r3, r4, r5, local, send, recv,
+):
     space, scene = lax.axis_index("space"), lax.axis_index("scene")
     core, x = scene % 2, scene // 2
     y, low, high = space % 2, (space // 2) % 2, space // 4
@@ -160,6 +162,37 @@
         pl.semaphore_signal(barrier, inc=1, device_id=device, device_id_type=MESH)
     pl.semaphore_wait(barrier, 5)
 
+    moves = []
+    for n, (source, target) in enumerate(
+        ((hid_source, hid_copies), (weight_source, weight), (grad_source, grad_copies), (weight_t_source, weight_t))
+    ):
+        moves.append(pltpu.make_async_copy(source, target, local.at[n]))
+        moves[n].start()
+
+    def convolve(n):
+        task, part = n // 3, n % 3
+        forward, b = task < bricks, task % bricks
+        copied, matrix = (hid_copies, weight) if forward else (grad_copies, weight_t)
+        if part == 0:
+            if b == 0:
+                for move in moves[:2] if forward else moves[2:]:
+                    move.wait()
+            total[...] = jnp.zeros_like(total)
+
+        def step(i, carry):
+            rows = copied[i % 3, b, pl.ds(pl.multiple_of((i // 3) * 64, 64), 512), :]
+            total[...] += jnp.dot(rows, matrix[i], preferred_element_type=jnp.float32)
+            return carry
+
+        lax.fori_loop(3 * part, 3 * part + 3, step, 0)
+        if part == 2 and forward:
+            summed = (features[b].astype(jnp.float32) + total[...]) * active[b]
+            outputs[b] = summed.astype(jnp.bfloat16)
+        elif part == 2:
+            kept = jnp.where(hidden[b].astype(jnp.float32) > 0, total[...], 0.0)
+            input_grad[b] = (grad[b].astype(jnp.float32) + kept).astype(jnp.bfloat16)
+
+    bricks = features.shape[0]
     chunks = r0.shape[0]
     copies = {}
 
@@ -211,43 +244,87 @@
     ahead = 2
     for k in range(min(ahead, chunks)):
         advance(0, k)
-    for at in range(chunks + 6):
+    parts = 6 * bricks
+    for at in range(chunks + 5 * LAG):
         if at + ahead < chunks:
             advance(0, at + ahead)
         for stage in range(1, 7):
-            k = at - (stage - 1)
+            k = at - LAG * (stage - 1)
             if 0 <= k < chunks:
                 advance(stage, k)
+        if 1 <= at <= parts:
+            convolve(at - 1)
+    for n in range(chunks + 5 * LAG - 1, parts):
+        convolve(n)
     for copy in copies.values():
         copy.wait_send()
 
 
-def scatter_sum(terms, scale):
+def scatter_sum(terms, scale, fields, streamed):
     taps, _, channels, half = terms.shape
+    features = fields[0]
     rows = channels // 16
     chunks = taps // GROUP
-    vmem = pl.BlockSpec(memory_space=pltpu.VMEM)
     f32 = jnp.float32
     tail = (rows, half)
     return pl.pallas_call(
         functools.partial(scatter_kernel, scale),
-        out_shape=jax.ShapeDtypeStruct((taps, 2 * rows, half // 2), f32),
-        in_specs=[vmem],
-        out_specs=vmem,
-        scratch_shapes=[
+        out_shape=(
+            jax.ShapeDtypeStruct(features.shape, jnp.bfloat16),
+            jax.ShapeDtypeStruct(features.shape, jnp.bfloat16),
+            jax.ShapeDtypeStruct((taps, 2 * rows, half // 2), f32),
+        ),
+        in_specs=vmem_specs(5) + [pl.BlockSpec(memory_space=pl.ANY)] * 4,
+        out_specs=tuple(vmem_specs(3)),
+        scratch_shapes=[pltpu.VMEM(array.shape, array.dtype) for array in streamed]
+        + [
+            pltpu.VMEM(features.shape[1:], f32),
             pltpu.VMEM((chunks, GROUP, 2, 2, 2, 2) + tail, f32),
             pltpu.VMEM((chunks, GROUP, 2, 2, 2) + tail, f32),
             pltpu.VMEM((chunks, GROUP, 2, 2) + tail, f32),
             pltpu.VMEM((chunks, GROUP, 2) + tail, f32),
             pltpu.VMEM((chunks, GROUP) + tail, f32),
             pltpu.VMEM((chunks, GROUP) + tail, f32),
+            pltpu.SemaphoreType.DMA((4,)),
             pltpu.SemaphoreType.DMA((6, chunks)),
             pltpu.SemaphoreType.DMA((6, chunks)),
         ],
         compiler_params=pltpu.CompilerParams(
             collective_id=0, has_side_effects=True, vmem_limit_bytes=VMEM_BYTES
         ),
-    )(terms.reshape(taps, 2, 2, 2, 2, 2, rows, half))
+    )(terms.reshape(taps, 2, 2, 2, 2, 2, rows, half), *fields, *streamed)
+
+
+def conv_kernel(features, active, hidden, grad, hid_copies, grad_copies, weight, weight_t, outputs, input_grad, total):
+    for b in range(features.shape[0]):
+        for copied, matrix in ((hid_copies, weight), (grad_copies, weight_t)):
+            total[...] = jnp.zeros_like(total)
+
+            def step(i, carry, b=b, copied=copied, matrix=matrix):
+                rows = copied[i % 3, b, pl.ds(pl.multiple_of((i // 3) * 64, 64), 512), :]
+                total[...] += jnp.dot(rows, matrix[i], preferred_element_type=jnp.float32)
+                return carry
+
+            lax.fori_loop(0, 9, step, 0)
+            if copied is hid_copies:
+                summed = (features[b].astype(jnp.float32) + total[...]) * active[b]
+                outputs[b] = summed.astype(jnp.bfloat16)
+            else:
+                kept = jnp.where(hidden[b].astype(jnp.float32) > 0, total[...], 0.0)
+                input_grad[b] = (grad[b].astype(jnp.float32) + kept).astype(jnp.bfloat16)
+
+
+def convolve_alone(fields, streamed):
+    shape = jax.ShapeDtypeStruct(fields[0].shape, jnp.bfloat16)
+    hid_copies, weight, grad_copies, weight_t = streamed
+    return pl.pallas_call(
+        conv_kernel,
+        out_shape=(shape, shape),
+        in_specs=vmem_specs(8),
+        out_specs=tuple(vmem_specs(2)),
+        scratch_shapes=[pltpu.VMEM(fields[0].shape[1:], jnp.float32)],
+        compiler_params=pltpu.CompilerParams(vmem_limit_bytes=VMEM_BYTES),
+    )(*fields, hid_copies, grad_copies, weight, weight_t)
 
 
 def per_device(features, cotangent, weight, counts, neighbours, occupancy):
@@ -268,16 +345,16 @@
     centre = (bricks + jnp.arange(bricks, dtype=jnp.int32))[:, None]
     lookup = jnp.concatenate([local_ids[:, :13], centre, local_ids[:, 13:]], axis=1)
     weight_t = weight[::-1].swapaxes(1, 2).reshape(9, 3 * channels, channels)
-    outputs, input_grad, terms = convolve(
-        lookup, feats, active.astype(jnp.float32), hidden.swapaxes(1, 2),
-        (hid_left, hidden, hid_right), (grad_left, grad, grad_right),
-        weight.reshape(9, 3 * channels, channels), weight_t,
-    )
+    terms, grad_copies = gradient_terms(lookup, hidden.swapaxes(1, 2), (grad_left, grad, grad_right))
+    hid_copies = halo_blocks(lookup, (hid_left, hidden, hid_right))
+    fields = (feats, active.astype(jnp.float32), hidden, grad)
+    streamed = (hid_copies, weight.reshape(9, 3 * channels, channels), grad_copies, weight_t)
     space, scene = lax.axis_size("space"), lax.axis_size("scene")
     scale = float(scene * space * bricks * voxels) ** (-0.5)
     if (space, scene) == (8, 4):
-        weight_grad = scatter_sum(terms, scale)
+        outputs, input_grad, weight_grad = scatter_sum(terms, scale, fields, streamed)
     else:
+        outputs, input_grad = convolve_alone(fields, streamed)
         whole = jnp.concatenate([terms[:, 0], terms[:, 1]], axis=2) * scale
         across = lax.psum_scatter(whole, "scene", scatter_dimension=2, tiled=True)
         weight_grad = lax.psum_scatter(across, "space", scatter_dimension=1, tiled=True)

time: 147 us -> 134 us (0.912)
  Pallas kernels: 89.6 us -> 73.3 us
  local copies, waits for them, and re-layouts: 10.8 us -> 14.5 us
    pallas_call x2 -> x3, Pallas kernels: 89.6 us -> 73.3 us  [the longest x1 52.8 us: scatter_sum(): pl.pallas_call(functools.partial(scatter_kernel, scale), out_shape=(jax.S...]
    unnamed x3 -> x5, local copies, waits for them, and re-layouts: 1.81 us -> 5.57 us
    ppermute x2, waiting for transfers between devices: 0.01 us -> 1.99 us  [both_sides(): right = lax.ppermute(cells, 'space', [(i + 1, i) for i in range(ends)])]
    ppermute x2, waiting for transfers between devices: 25.3 us -> 23.4 us  [both_sides(): left = lax.ppermute(cells, 'space', [(i, i + 1) for i in range(ends)])]
  transfers between devices with their start and end apart: 4 -> 4, of which waited for: 2 -> 2; matrix products, arithmetic and copies ran while one was open for 8% -> 9% of each run, Pallas kernels for 0% -> 5%
where the time goes in v2:
time: 134 us
  Pallas kernels  73.3 us (55%)
  waiting for transfers between devices  25.3 us (19%)
  local copies, waits for them, and re-layouts  14.5 us (11%)
  starting transfers between devices  12.9 us (10%)
  other arithmetic  6.4 us (5%)
    pallas_call x1, Pallas kernels, scatter_sum(): pl.pallas_call(functools.partial(scatter_kernel, scale), out_shape=(jax.S...  52.8 us
    ppermute x2, waiting for transfers between devices, both_sides(): left = lax.ppermute(cells, 'space', [(i, i + 1) for i in range(ends)])  23.4 us
    pallas_call x1, Pallas kernels, gradient_terms(): pl.pallas_call(gradient_kernel, out_shape=(jax.ShapeDtypeStruct((27, 2, c...  13.9 us
    ppermute x2, starting transfers between devices, both_sides(): left = lax.ppermute(cells, 'space', [(i, i + 1) for i in range(ends)])  10.4 us
    pallas_call x1, Pallas kernels, halo_blocks(): pl.pallas_call(blocks_kernel, out_shape=jax.ShapeDtypeStruct((3, bricks,...  6.71 us
    transpose x2, local copies, waits for them, and re-layouts, per_device(): weight_t = weight[::-1].swapaxes(1, 2).reshape(9, 3 * channels, channels)  5.78 us
    unnamed x5, local copies, waits for them, and re-layouts  5.57 us
  transfers between devices with their start and end apart: 4, of which 2 were waited for; matrix products, arithmetic and copies ran while one was open for 9% of the time, Pallas kernels for 5%

profile of v2, /device:TPU:1, one launch (start us, length us, event | category | flops | bytes accessed | tf_op | source)
XLA Modules:
  0.0 133.8 jit_solution(3097172582779907898)
XLA Ops:
  1.3 0.8 fusion
  2.0 2.4 %broadcast_multiply_fusion = (bf16[2,512,256]{2,1,0:T(8,128)(2,1)}, bf16[2,512,256]{2,1,0:T(8,128)(2,1)}) fusion(bf16[2,512,256]{2,1,0:T(8,128)(2,1)} %bitcast.24, bf16[2,512]{1,0:T(2,128)(2,1)S(1)} %fusion, bf16[2,512,256]{2,1,0:T(8,128)(2,1)} %bitcast.22), kind=kLoop, calls=%fused_computation.3 | loop fusion | flops 786432 | bytes 2099200 | tf_op jit(solution)/shard_map/mul | solution.py:338
  4.4 1.3 collective-permute-start.1
  5.7 5.4 %collective-permute-start = (bf16[2,512,256]{2,1,0:T(8,128)(2,1)}, bf16[2,512,256]{2,1,0:T(8,128)(2,1)}, u32[]{:S(2)}, u32[]{:S(2)}) collective-permute-start(bf16[2,512,256]{2,1,0:T(8,128)(2,1)} %get-tuple-element.13.grad), channel_id=1, source_target_pairs={{0,4},{4,8},{8,12},{12,16},{16,20},{20,24},{24,28},{1,5},{5,9},{9,... | collective-permute-start | bytes 1572872 | tf_op jit(solution)/shard_map/ppermute | solution.py:19
  11.1 1.3 collective-permute-start.3
  12.4 4.9 %collective-permute-start.2 = (bf16[2,512,256]{2,1,0:T(8,128)(2,1)}, bf16[2,512,256]{2,1,0:T(8,128)(2,1)}, u32[]{:S(2)}, u32[]{:S(2)}) collective-permute-start(bf16[2,512,256]{2,1,0:T(8,128)(2,1)} %get-tuple-element.14.hidden), channel_id=1, source_target_pairs={{0,4},{4,8},{8,12},{12,16},{16,20},{20,24},{24,28},{1,5},{5,9},{9,... | collective-permute-start | bytes 1572872 | tf_op jit(solution)/shard_map/ppermute | solution.py:19
  17.4 0.7 fusion.1
  18.0 0.1 fusion.2
  18.1 0.0 copy-start
  18.1 2.2 %reverse_bitcast_fusion = bf16[27,256,256]{1,2,0:T(8,128)(2,1)S(1)} fusion(bf16[27,256,256]{2,1,0:T(8,128)(2,1)} %param.8), kind=kLoop, calls=%fused_computation | loop fusion | bytes 7077888 | tf_op jit(solution)/shard_map/transpose | solution.py:347
  20.4 0.0 copy-done
  20.4 1.0 copy.15
  21.4 2.1 %copy.14.hidden_t = bf16[2,256,512]{2,1,0:T(8,128)(2,1)} copy(bf16[2,256,512]{1,2,0:T(8,128)(2,1)} %bitcast.4) | data formatting | bytes 1048576 | tf_op jit(solution)/shard_map/transpose | solution.py:348
  23.5 3.5 %copy.17 = bf16[27,256,256]{2,1,0:T(8,128)(2,1)} copy(bf16[27,256,256]{1,2,0:T(8,128)(2,1)S(1)} %reverse_bitcast_fusion) | data formatting | bytes 7077888 | tf_op jit(solution)/shard_map/transpose | solution.py:347
  27.0 0.6 pad_add_fusion.lookup
  27.7 1.9 %multiply_convert_fusion.active = f32[2,512,1]{2,1,0:T(8,128)} fusion(s32[2,512,1]{2,1,0:T(8,128)} %copy.15, s32[2]{0:T(128)S(1)} %compare_convert_fusion), kind=kLoop, calls=%fused_computation.1 | loop fusion | flops 2048 | bytes 8200 | tf_op jit(solution)/shard_map/convert_element_type | solution.py:350
  29.6 2.0 %collective-permute-done.3.right = bf16[2,512,256]{2,1,0:T(8,128)(2,1)} collective-permute-done((bf16[2,512,256]{2,1,0:T(8,128)(2,1)}, bf16[2,512,256]{2,1,0:T(8,128)(2,1)}, u32[]{:S(2)}, u32[]{:S(2)}) %collective-permute-start.3) | collective-permute-done | bytes 524320 | tf_op jit(solution)/shard_map/ppermute | solution.py:20
  31.6 23.4 %collective-permute-done.2.left = bf16[2,512,256]{2,1,0:T(8,128)(2,1)} collective-permute-done((bf16[2,512,256]{2,1,0:T(8,128)(2,1)}, bf16[2,512,256]{2,1,0:T(8,128)(2,1)}, u32[]{:S(2)}, u32[]{:S(2)}) %collective-permute-start.2) | collective-permute-done | bytes 524320 | tf_op jit(solution)/shard_map/ppermute | solution.py:19
  54.9 6.7 %shard_map.86.hid_source = bf16[3,2,640,768]{3,2,1,0:T(8,128)(2,1)} custom-call(s32[2,27]{1,0:T(2,128)} %pad_add_fusion.lookup, bf16[2,512,256]{2,1,0:T(8,128)(2,1)} %collective-permute-done.2.left, bf16[2,512,256]{2,1,0:T(8,128)(2,1)} %get-tuple-element.14.hidden, bf16[2,512,256]{2,1,0:T(8,128)(2,1)} %collective-permute-done.3.right), custom_call_target="tpu_custom_call" | custom-call | bytes 30000000 | tf_op jit(solution)/shard_map/pallas_call | solution.py:133
  61.7 0.0 collective-permute-done.1.right
  61.7 0.0 collective-permute-done.left
  61.7 13.9 %shard_map.85 = (f32[27,2,256,128]{3,2,1,0:T(8,128)}, bf16[3,2,640,768]{3,2,1,0:T(8,128)(2,1)}) custom-call(s32[2,27]{1,0:T(2,128)} %pad_add_fusion.lookup, bf16[2,256,512]{2,1,0:T(8,128)(2,1)} %copy.14.hidden_t, bf16[2,512,256]{2,1,0:T(8,128)(2,1)} %collective-permute-done.left, bf16[2,512,256]{2,1,0:T(8,128)(2,1)} %get-tuple-element.13.grad, ...), custom_call_target="tpu_custom_call" | custom-call | flops 3623878656 | bytes 60000000 | tf_op jit(solution)/shard_map/pallas_call | solution.py:115
  75.5 52.8 %shard_map.87 = (bf16[2,512,256]{2,1,0:T(8,128)(2,1)}, bf16[2,512,256]{2,1,0:T(8,128)(2,1)}, f32[27,32,64]{2,1,0:T(8,128)}) custom-call(f32[27,2,2,2,2,2,16,128]{7,6,5,4,3,2,1,0:T(8,128)} %bitcast.21, bf16[2,512,256]{2,1,0:T(8,128)(2,1)} %bitcast.23, f32[2,512,1]{2,1,0:T(8,128)} %multiply_convert_fusion.active, ...), custom_call_target="tpu_custom_call" | custom-call | tf_op jit(solution)/shard_map/pallas_call | solution.py:270
  128.3 1.9 %copy.22 = bf16[1,2,8,8,8,256]{5,4,3,2,1,0:T(8,128)(2,1)} copy(bf16[1,2,8,8,8,256]{5,4,3,2,1,0:T(8,128)(2,1)} %bitcast.26) | data formatting | bytes 1048576
  130.2 1.9 %copy.23 = bf16[1,2,8,8,8,256]{5,4,3,2,1,0:T(8,128)(2,1)} copy(bf16[1,2,8,8,8,256]{5,4,3,2,1,0:T(8,128)(2,1)} %bitcast.25) | data formatting | bytes 1048576
  132.0 1.8 %copy.24 = f32[27,32,64]{2,1,0:T(8,128)} copy(f32[27,32,64]{2,1,0:T(8,128)} %get-tuple-element.22) | data formatting | bytes 442368
  (2 shorter events, 0.0 us)
Async XLA Ops:
  4.4 57.2 %collective-permute-start.1 = (bf16[2,512,256]{2,1,0:T(8,128)(2,1)}, bf16[2,512,256]{2,1,0:T(8,128)(2,1)}, u32[]{:S(2)}, u32[]{:S(2)}) collective-permute-start(bf16[2,512,256]{2,1,0:T(8,128)(2,1)} %get-tuple-element.13.grad), channel_id=1, source_target_pairs={{4,0},{8,4},{12,8},{16,12},{20,16},{24,20},{28,24},{5,1},{9,5},{13... | collective-permute-start | bytes 1572872 | tf_op jit(solution)/shard_map/ppermute | solution.py:20
  5.7 55.9 %collective-permute-start = (bf16[2,512,256]{2,1,0:T(8,128)(2,1)}, bf16[2,512,256]{2,1,0:T(8,128)(2,1)}, u32[]{:S(2)}, u32[]{:S(2)}) collective-permute-start(bf16[2,512,256]{2,1,0:T(8,128)(2,1)} %get-tuple-element.13.grad), channel_id=1, source_target_pairs={{0,4},{4,8},{8,12},{12,16},{16,20},{20,24},{24,28},{1,5},{5,9},{9,... | collective-permute-start | bytes 1572872 | tf_op jit(solution)/shard_map/ppermute | solution.py:19
  11.1 20.4 %collective-permute-start.3 = (bf16[2,512,256]{2,1,0:T(8,128)(2,1)}, bf16[2,512,256]{2,1,0:T(8,128)(2,1)}, u32[]{:S(2)}, u32[]{:S(2)}) collective-permute-start(bf16[2,512,256]{2,1,0:T(8,128)(2,1)} %get-tuple-element.14.hidden), channel_id=1, source_target_pairs={{4,0},{8,4},{12,8},{16,12},{20,16},{24,20},{28,24},{5,1},{9,5},{13... | collective-permute-start | bytes 1572872 | tf_op jit(solution)/shard_map/ppermute | solution.py:20
  12.4 42.5 %collective-permute-start.2 = (bf16[2,512,256]{2,1,0:T(8,128)(2,1)}, bf16[2,512,256]{2,1,0:T(8,128)(2,1)}, u32[]{:S(2)}, u32[]{:S(2)}) collective-permute-start(bf16[2,512,256]{2,1,0:T(8,128)(2,1)} %get-tuple-element.14.hidden), channel_id=1, source_target_pairs={{0,4},{4,8},{8,12},{12,16},{16,20},{20,24},{24,28},{1,5},{5,9},{9,... | collective-permute-start | bytes 1572872 | tf_op jit(solution)/shard_map/ppermute | solution.py:19
  18.1 2.2 %copy-start = (s32[1,2,512]{2,1,0:T(2,128)S(1)}, s32[1,2,512]{2,1,0:T(2,128)}, u32[]{:S(2)}) copy-start(s32[1,2,512]{2,1,0:T(2,128)} %param.11) | copy-start | bytes 12292

commit v3 on v2

--- a/solution.py
+++ b/solution.py
@@ -37,17 +37,70 @@
     return slice(0, 1), slice(16, 17)
 
 
+def prepare_kernel(features, cotangent, active, hidden, grad, packed_hidden, packed_grad, block):
+    channels = block.shape[-1]
+    for b in range(features.shape[0]):
+        for source, target, packed in ((cotangent, grad, packed_grad), (features, hidden, packed_hidden)):
+
+            def mask(x, carry, source=source, target=target, b=b):
+                at = pl.ds(pl.multiple_of(x * 64, 64), 64)
+                rows = source[b, at, :].astype(jnp.float32)
+                if source is features:
+                    rows = jnp.maximum(rows, 0)
+                rows = rows * active[b, at, :]
+                target[b, at, :] = rows.astype(jnp.bfloat16)
+                block[x] = rows.reshape(8, 8, channels)
+                return carry
+
+            lax.fori_loop(0, 8, mask, 0)
+            for n, x in enumerate((0, 7)):
+                packed[b, 64 * n : 64 * n + 64, :] = block[x].reshape(64, channels).astype(jnp.bfloat16)
+            for x in range(1, 7):
+                faces_y = jnp.concatenate([block[x, 0], block[x, 7]], axis=0)
+                packed[b, 112 + 16 * x : 128 + 16 * x, :] = faces_y.astype(jnp.bfloat16)
+                faces_z = jnp.concatenate([block[x, :, 0, :], block[x, :, 7, :]], axis=0)
+                packed[b, 208 + 16 * x : 224 + 16 * x, :] = faces_z.astype(jnp.bfloat16)
+
+
+def prepare(features, cotangent, active):
+    bricks, _, channels = features.shape
+    whole = jax.ShapeDtypeStruct(features.shape, jnp.bfloat16)
+    surface = jax.ShapeDtypeStruct((bricks, 320, channels), jnp.bfloat16)
+    return pl.pallas_call(
+        prepare_kernel,
+        out_shape=(whole, whole, surface, surface),
+        in_specs=vmem_specs(3),
+        out_specs=tuple(vmem_specs(4)),
+        scratch_shapes=[pltpu.VMEM((8, 8, 8, channels), jnp.float32)],
+        compiler_params=pltpu.CompilerParams(vmem_limit_bytes=VMEM_BYTES),
+    )(features, cotangent, active)
+
+
+def unpack(packed, b, at, window):
+    channels = window.shape[-1]
+    for n, x in enumerate((0, 7)):
+        rows = packed[b, 64 * n : 64 * n + 64, :].astype(jnp.float32)
+        window[at, x] = rows.reshape(8, 8, channels)
+    for x in range(1, 7):
+        faces_y = packed[b, 112 + 16 * x : 128 + 16 * x, :].astype(jnp.float32)
+        faces_z = packed[b, 208 + 16 * x : 224 + 16 * x, :].astype(jnp.float32)
+        window[at, x, 0], window[at, x, 7] = faces_y[:8], faces_y[8:]
+        window[at, x, :, 0, :], window[at, x, :, 7, :] = faces_z[:8], faces_z[8:]
+
+
 def fill_copies(lookup, bricks, sides, window, staged, copies):
     channels = staged.shape[-1]
-    for side, ref in enumerate(sides):
-        for b in range(bricks):
-
-            def widen(x, carry, ref=ref, b=b, at=side * bricks + b):
-                rows = ref[b, pl.ds(pl.multiple_of(x * 64, 64), 64), :]
-                window[at, x] = rows.astype(jnp.float32).reshape(8, 8, channels)
-                return carry
-
-            lax.fori_loop(0, 8, widen, 0)
+    left, own, right = sides
+    for b in range(bricks):
+        unpack(left, b, b, window)
+        unpack(right, b, 2 * bricks + b, window)
+
+        def widen(x, carry, b=b):
+            rows = own[b, pl.ds(pl.multiple_of(x * 64, 64), 64), :]
+            window[bricks + b, x] = rows.astype(jnp.float32).reshape(8, 8, channels)
+            return carry
+
+        lax.fori_loop(0, 8, widen, 0)
     for b in range(bricks):
         for sx in (-1, 0, 1):
             for sy in (-1, 0, 1):
@@ -334,11 +387,12 @@
     feats = features.reshape(bricks, voxels, channels)
     slot_live = (jnp.arange(bricks, dtype=jnp.int32) < counts[0, 0]).astype(jnp.int32)
     active = (occupancy[0] * slot_live[:, None]).reshape(bricks, voxels, 1)
-    live = active.astype(jnp.bfloat16)
-    grad = cotangent.reshape(bricks, voxels, channels) * live
-    hidden = jnp.maximum(feats, 0) * live
-    grad_left, grad_right = both_sides(grad)
-    hid_left, hid_right = both_sides(hidden)
+    live = active.astype(jnp.float32)
+    hidden, grad, packed_hidden, packed_grad = prepare(
+        feats, cotangent.reshape(bricks, voxels, channels), live
+    )
+    grad_left, grad_right = both_sides(packed_grad)
+    hid_left, hid_right = both_sides(packed_hidden)
     first_id = (lax.axis_index("space") - 1) * bricks
     linked = neighbours[0]
     local_ids = jnp.where(linked >= 0, linked - first_id, -1)
@@ -347,7 +401,7 @@
     weight_t = weight[::-1].swapaxes(1, 2).reshape(9, 3 * channels, channels)
     terms, grad_copies = gradient_terms(lookup, hidden.swapaxes(1, 2), (grad_left, grad, grad_right))
     hid_copies = halo_blocks(lookup, (hid_left, hidden, hid_right))
-    fields = (feats, active.astype(jnp.float32), hidden, grad)
+    fields = (feats, live, hidden, grad)
     streamed = (hid_copies, weight.reshape(9, 3 * channels, channels), grad_copies, weight_t)
     space, scene = lax.axis_size("space"), lax.axis_size("scene")
     scale = float(scene * space * bricks * voxels) ** (-0.5)

time: 134 us -> 121 us (0.903)
  waiting for transfers between devices: 25.3 us -> 12.2 us
  other arithmetic: 6.4 us -> 1.58 us
  Pallas kernels: 73.3 us -> 78 us
    ppermute x2, waiting for transfers between devices: 23.4 us -> 12.2 us  [both_sides(): left = lax.ppermute(cells, 'space', [(i, i + 1) for i in range(ends)])]
    pallas_call x0 -> x1, Pallas kernels: none -> 5.11 us  [prepare(): pl.pallas_call(prepare_kernel, out_shape=(whole, whole, surface, surface)...]
    mul x1 -> x0, other arithmetic: 2.37 us -> none  [per_device(): grad = cotangent.reshape(bricks, voxels, channels) * live]
    transpose x1 -> x0, local copies, waits for them, and re-layouts: 2.07 us -> none  [per_device(): hidden.swapaxes(1, 2)]
    pallas_call x0 -> x1, local copies, waits for them, and re-layouts: none -> 2.06 us  [prepare(): pl.pallas_call(prepare_kernel, out_shape=(whole, whole, surface, surface)...]
    ppermute x2, waiting for transfers between devices: 1.99 us -> 0.01 us  [both_sides(): right = lax.ppermute(cells, 'space', [(i + 1, i) for i in range(ends)])]
    convert_element_type x2 -> x1, other arithmetic: 2.7 us -> 0.9 us  [per_device(): live = active.astype(jnp.float32)]
  transfers between devices with their start and end apart: 4 -> 4, of which waited for: 2 -> 1; matrix products, arithmetic and copies ran while one was open for 9% -> 7% of each run, Pallas kernels for 5% -> 5%
where the time goes in v3:
time: 121 us; the launch traced here: 120 us
  Pallas kernels  78 us (64%)
  local copies, waits for them, and re-layouts  14.4 us (12%)
  starting transfers between devices  12.8 us (11%)
  waiting for transfers between devices  12.2 us (10%)
  other arithmetic  1.58 us (1%)
  between operations  1.34 us (1%)
    pallas_call x1, Pallas kernels, scatter_sum(): pl.pallas_call(functools.partial(scatter_kernel, scale), out_shape=(jax.S...  52.7 us
    pallas_call x1, Pallas kernels, gradient_terms(): pl.pallas_call(gradient_kernel, out_shape=(jax.ShapeDtypeStruct((27, 2, c...  13.7 us
    ppermute x2, waiting for transfers between devices, both_sides(): left = lax.ppermute(cells, 'space', [(i, i + 1) for i in range(ends)])  12.2 us
    ppermute x2, starting transfers between devices, both_sides(): left = lax.ppermute(cells, 'space', [(i, i + 1) for i in range(ends)])  10.3 us
    pallas_call x1, Pallas kernels, halo_blocks(): pl.pallas_call(blocks_kernel, out_shape=jax.ShapeDtypeStruct((3, bricks,...  6.51 us
    transpose x2, local copies, waits for them, and re-layouts, per_device(): weight_t = weight[::-1].swapaxes(1, 2).reshape(9, 3 * channels, channels)  5.79 us
    unnamed x5, local copies, waits for them, and re-layouts  5.57 us
    pallas_call x1, Pallas kernels, prepare(): pl.pallas_call(prepare_kernel, out_shape=(whole, whole, surface, surface)...  5.11 us
  transfers between devices with their start and end apart: 4, of which 1 were waited for; matrix products, arithmetic and copies ran while one was open for 7% of the time, Pallas kernels for 5%

profile of v3, /device:TPU:1, one launch (start us, length us, event | category | flops | bytes accessed | tf_op | source)
XLA Modules:
  0.0 120.3 jit_solution(10547186032892872523)
XLA Ops:
  1.3 0.9 copy.14
  2.2 0.9 multiply_convert_fusion.active
  3.1 5.1 %shard_map.85 = (bf16[2,512,256]{2,1,0:T(8,128)(2,1)}, bf16[2,512,256]{2,1,0:T(8,128)(2,1)}, bf16[2,320,256]{2,1,0:T(8,128)(2,1)}, bf16[2,320,256]{2,1,0:T(8,128)(2,1)}) custom-call(bf16[2,512,256]{2,1,0:T(8,128)(2,1)} %bitcast.18, bf16[2,512,256]{2,1,0:T(8,128)(2,1)} %bitcast.20, f32[2,512,1]{2,1,0:T(8,128)} %multiply_convert_fusion.active), custom_call_target="tpu_custom_call" | custom-call | tf_op jit(solution)/shard_map/pallas_call | solution.py:69
  8.2 1.3 %collective-permute-start.1 = (bf16[2,320,256]{2,1,0:T(8,128)(2,1)}, bf16[2,320,256]{2,1,0:T(8,128)(2,1)}, u32[]{:S(2)}, u32[]{:S(2)}) collective-permute-start(bf16[2,320,256]{2,1,0:T(8,128)(2,1)} %get-tuple-element.13), channel_id=1, source_target_pairs={{4,0},{8,4},{12,8},{16,12},{20,16},{24,20},{28,24},{5,1},{9,5},{13... | collective-permute-start | bytes 983048 | tf_op jit(solution)/shard_map/ppermute | solution.py:20
  9.5 5.3 %collective-permute-start = (bf16[2,320,256]{2,1,0:T(8,128)(2,1)}, bf16[2,320,256]{2,1,0:T(8,128)(2,1)}, u32[]{:S(2)}, u32[]{:S(2)}) collective-permute-start(bf16[2,320,256]{2,1,0:T(8,128)(2,1)} %get-tuple-element.13), channel_id=1, source_target_pairs={{0,4},{4,8},{8,12},{12,16},{16,20},{20,24},{24,28},{1,5},{5,9},{9,... | collective-permute-start | bytes 983048 | tf_op jit(solution)/shard_map/ppermute | solution.py:19
  14.8 1.3 %collective-permute-start.3 = (bf16[2,320,256]{2,1,0:T(8,128)(2,1)}, bf16[2,320,256]{2,1,0:T(8,128)(2,1)}, u32[]{:S(2)}, u32[]{:S(2)}) collective-permute-start(bf16[2,320,256]{2,1,0:T(8,128)(2,1)} %get-tuple-element.16), channel_id=1, source_target_pairs={{4,0},{8,4},{12,8},{16,12},{20,16},{24,20},{28,24},{5,1},{9,5},{13... | collective-permute-start | bytes 983048 | tf_op jit(solution)/shard_map/ppermute | solution.py:20
  16.1 4.9 %collective-permute-start.2 = (bf16[2,320,256]{2,1,0:T(8,128)(2,1)}, bf16[2,320,256]{2,1,0:T(8,128)(2,1)}, u32[]{:S(2)}, u32[]{:S(2)}) collective-permute-start(bf16[2,320,256]{2,1,0:T(8,128)(2,1)} %get-tuple-element.16), channel_id=1, source_target_pairs={{0,4},{4,8},{8,12},{12,16},{16,20},{20,24},{24,28},{1,5},{5,9},{9,... | collective-permute-start | bytes 983048 | tf_op jit(solution)/shard_map/ppermute | solution.py:19
  21.1 2.1 %copy.16 = bf16[2,512,256]{1,2,0:T(8,128)(2,1)} copy(bf16[2,512,256]{2,1,0:T(8,128)(2,1)} %get-tuple-element.12.hidden) | data formatting | bytes 1048576 | tf_op jit(solution)/shard_map/pallas_call | solution.py:69
  23.1 2.2 %reverse_bitcast_fusion = bf16[27,256,256]{1,2,0:T(8,128)(2,1)S(1)} fusion(bf16[27,256,256]{2,1,0:T(8,128)(2,1)} %param.8), kind=kLoop, calls=%fused_computation | loop fusion | bytes 7077888 | tf_op jit(solution)/shard_map/transpose | solution.py:401
  25.4 0.0 copy-start
  25.4 3.6 %copy.17 = bf16[27,256,256]{2,1,0:T(8,128)(2,1)} copy(bf16[27,256,256]{1,2,0:T(8,128)(2,1)S(1)} %reverse_bitcast_fusion) | data formatting | bytes 7077888 | tf_op jit(solution)/shard_map/transpose | solution.py:401
  28.9 0.0 copy-done
  28.9 0.1 fusion.1
  29.0 0.7 pad_add_fusion.lookup
  29.7 0.0 collective-permute-done.3.right
  29.7 12.2 %collective-permute-done.2.left = bf16[2,320,256]{2,1,0:T(8,128)(2,1)} collective-permute-done((bf16[2,320,256]{2,1,0:T(8,128)(2,1)}, bf16[2,320,256]{2,1,0:T(8,128)(2,1)}, u32[]{:S(2)}, u32[]{:S(2)}) %collective-permute-start.2) | collective-permute-done | bytes 327712 | tf_op jit(solution)/shard_map/ppermute | solution.py:19
  41.9 6.5 %shard_map.87.hid_source = bf16[3,2,640,768]{3,2,1,0:T(8,128)(2,1)} custom-call(s32[2,27]{1,0:T(2,128)} %pad_add_fusion.lookup, bf16[2,320,256]{2,1,0:T(8,128)(2,1)} %collective-permute-done.2.left, bf16[2,512,256]{2,1,0:T(8,128)(2,1)} %get-tuple-element.12.hidden, bf16[2,320,256]{2,1,0:T(8,128)(2,1)} %collective-permute-done.3.right), custom_call_target="tpu_custom_call" | custom-call | bytes 30000000 | tf_op jit(solution)/shard_map/pallas_call | solution.py:186
  48.4 0.0 collective-permute-done.1.right
  48.4 0.0 collective-permute-done.left
  48.4 13.7 %shard_map.86 = (f32[27,2,256,128]{3,2,1,0:T(8,128)}, bf16[3,2,640,768]{3,2,1,0:T(8,128)(2,1)}) custom-call(s32[2,27]{1,0:T(2,128)} %pad_add_fusion.lookup, bf16[2,256,512]{2,1,0:T(8,128)(2,1)} %bitcast.21, bf16[2,320,256]{2,1,0:T(8,128)(2,1)} %collective-permute-done.left, bf16[2,512,256]{2,1,0:T(8,128)(2,1)} %get-tuple-element.14.grad, ...), custom_call_target="tpu_custom_call" | custom-call | flops 3623878656 | bytes 60000000 | tf_op jit(solution)/shard_map/pallas_call | solution.py:168
  62.1 52.7 %shard_map.88 = (bf16[2,512,256]{2,1,0:T(8,128)(2,1)}, bf16[2,512,256]{2,1,0:T(8,128)(2,1)}, f32[27,32,64]{2,1,0:T(8,128)}) custom-call(f32[27,2,2,2,2,2,16,128]{7,6,5,4,3,2,1,0:T(8,128)} %bitcast.17, bf16[2,512,256]{2,1,0:T(8,128)(2,1)} %bitcast.19, f32[2,512,1]{2,1,0:T(8,128)} %multiply_convert_fusion.active, ...), custom_call_target="tpu_custom_call" | custom-call | tf_op jit(solution)/shard_map/pallas_call | solution.py:323
  114.8 1.9 %copy.22 = bf16[1,2,8,8,8,256]{5,4,3,2,1,0:T(8,128)(2,1)} copy(bf16[1,2,8,8,8,256]{5,4,3,2,1,0:T(8,128)(2,1)} %bitcast.23) | data formatting | bytes 1048576
  116.7 1.9 %copy.23 = bf16[1,2,8,8,8,256]{5,4,3,2,1,0:T(8,128)(2,1)} copy(bf16[1,2,8,8,8,256]{5,4,3,2,1,0:T(8,128)(2,1)} %bitcast.22) | data formatting | bytes 1048576
  118.5 1.8 %copy.24 = f32[27,32,64]{2,1,0:T(8,128)} copy(f32[27,32,64]{2,1,0:T(8,128)} %get-tuple-element.28) | data formatting | bytes 442368
  (3 shorter events, 0.0 us)
Async XLA Ops:
  8.2 40.2 %collective-permute-start.1 = (bf16[2,320,256]{2,1,0:T(8,128)(2,1)}, bf16[2,320,256]{2,1,0:T(8,128)(2,1)}, u32[]{:S(2)}, u32[]{:S(2)}) collective-permute-start(bf16[2,320,256]{2,1,0:T(8,128)(2,1)} %get-tuple-element.13), channel_id=1, source_target_pairs={{4,0},{8,4},{12,8},{16,12},{20,16},{24,20},{28,24},{5,1},{9,5},{13... | collective-permute-start | bytes 983048 | tf_op jit(solution)/shard_map/ppermute | solution.py:20
  9.5 38.9 %collective-permute-start = (bf16[2,320,256]{2,1,0:T(8,128)(2,1)}, bf16[2,320,256]{2,1,0:T(8,128)(2,1)}, u32[]{:S(2)}, u32[]{:S(2)}) collective-permute-start(bf16[2,320,256]{2,1,0:T(8,128)(2,1)} %get-tuple-element.13), channel_id=1, source_target_pairs={{0,4},{4,8},{8,12},{12,16},{16,20},{20,24},{24,28},{1,5},{5,9},{9,... | collective-permute-start | bytes 983048 | tf_op jit(solution)/shard_map/ppermute | solution.py:19
  14.8 14.8 %collective-permute-start.3 = (bf16[2,320,256]{2,1,0:T(8,128)(2,1)}, bf16[2,320,256]{2,1,0:T(8,128)(2,1)}, u32[]{:S(2)}, u32[]{:S(2)}) collective-permute-start(bf16[2,320,256]{2,1,0:T(8,128)(2,1)} %get-tuple-element.16), channel_id=1, source_target_pairs={{4,0},{8,4},{12,8},{16,12},{20,16},{24,20},{28,24},{5,1},{9,5},{13... | collective-permute-start | bytes 983048 | tf_op jit(solution)/shard_map/ppermute | solution.py:20
  16.1 25.7 %collective-permute-start.2 = (bf16[2,320,256]{2,1,0:T(8,128)(2,1)}, bf16[2,320,256]{2,1,0:T(8,128)(2,1)}, u32[]{:S(2)}, u32[]{:S(2)}) collective-permute-start(bf16[2,320,256]{2,1,0:T(8,128)(2,1)} %get-tuple-element.16), channel_id=1, source_target_pairs={{0,4},{4,8},{8,12},{12,16},{16,20},{20,24},{24,28},{1,5},{5,9},{9,... | collective-permute-start | bytes 983048 | tf_op jit(solution)/shard_map/ppermute | solution.py:19
  25.4 3.6 %copy-start = (s32[1,2,26]{2,1,0:T(2,128)S(1)}, s32[1,2,26]{2,1,0:T(2,128)}, u32[]{:S(2)}) copy-start(s32[1,2,26]{2,1,0:T(2,128)} %param.10) | copy-start | bytes 628

commit v4 on v3

--- a/solution.py
+++ b/solution.py
@@ -11,6 +11,7 @@
 VMEM_BYTES = 56 * 1024 * 1024
 GROUP = 3
 LAG = 2
+DELAY = 3
 
 
 def both_sides(cells):
@@ -37,10 +38,11 @@
     return slice(0, 1), slice(16, 17)
 
 
-def prepare_kernel(features, cotangent, active, hidden, grad, packed_hidden, packed_grad, block):
+def prepare_kernel(features, cotangent, active, hidden, grad, packed, block):
     channels = block.shape[-1]
-    for b in range(features.shape[0]):
-        for source, target, packed in ((cotangent, grad, packed_grad), (features, hidden, packed_hidden)):
+    bricks = features.shape[0]
+    for b in range(bricks):
+        for source, target, to in ((features, hidden, b), (cotangent, grad, bricks + b)):
 
             def mask(x, carry, source=source, target=target, b=b):
                 at = pl.ds(pl.multiple_of(x * 64, 64), 64)
@@ -54,23 +56,23 @@
 
             lax.fori_loop(0, 8, mask, 0)
             for n, x in enumerate((0, 7)):
-                packed[b, 64 * n : 64 * n + 64, :] = block[x].reshape(64, channels).astype(jnp.bfloat16)
+                packed[to, 64 * n : 64 * n + 64, :] = block[x].reshape(64, channels).astype(jnp.bfloat16)
             for x in range(1, 7):
                 faces_y = jnp.concatenate([block[x, 0], block[x, 7]], axis=0)
-                packed[b, 112 + 16 * x : 128 + 16 * x, :] = faces_y.astype(jnp.bfloat16)
+                packed[to, 112 + 16 * x : 128 + 16 * x, :] = faces_y.astype(jnp.bfloat16)
                 faces_z = jnp.concatenate([block[x, :, 0, :], block[x, :, 7, :]], axis=0)
-                packed[b, 208 + 16 * x : 224 + 16 * x, :] = faces_z.astype(jnp.bfloat16)
+                packed[to, 208 + 16 * x : 224 + 16 * x, :] = faces_z.astype(jnp.bfloat16)
 
 
 def prepare(features, cotangent, active):
     bricks, _, channels = features.shape
     whole = jax.ShapeDtypeStruct(features.shape, jnp.bfloat16)
-    surface = jax.ShapeDtypeStruct((bricks, 320, channels), jnp.bfloat16)
+    surface = jax.ShapeDtypeStruct((2 * bricks, 320, channels), jnp.bfloat16)
     return pl.pallas_call(
         prepare_kernel,
-        out_shape=(whole, whole, surface, surface),
+        out_shape=(whole, whole, surface),
         in_specs=vmem_specs(3),
-        out_specs=tuple(vmem_specs(4)),
+        out_specs=tuple(vmem_specs(3)),
         scratch_shapes=[pltpu.VMEM((8, 8, 8, channels), jnp.float32)],
         compiler_params=pltpu.CompilerParams(vmem_limit_bytes=VMEM_BYTES),
     )(features, cotangent, active)
@@ -88,12 +90,12 @@
         window[at, x, :, 0, :], window[at, x, :, 7, :] = faces_z[:8], faces_z[8:]
 
 
-def fill_copies(lookup, bricks, sides, window, staged, copies):
+def fill_copies(lookup, bricks, first, sides, window, staged, copies):
     channels = staged.shape[-1]
     left, own, right = sides
     for b in range(bricks):
-        unpack(left, b, b, window)
-        unpack(right, b, 2 * bricks + b, window)
+        unpack(left, first + b, b, window)
+        unpack(right, first + b, 2 * bricks + b, window)
 
         def widen(x, carry, b=b):
             rows = own[b, pl.ds(pl.multiple_of(x * 64, 64), 64), :]
@@ -130,7 +132,7 @@
     bricks = grad.shape[0]
     channels = grad.shape[-1]
     half = channels // 2
-    fill_copies(lookup, bricks, (left, grad, right), window, staged, copies)
+    fill_copies(lookup, bricks, bricks, (left, grad, right), window, staged, copies)
 
     def gradient(i, carry):
         for z in range(3):
@@ -149,7 +151,7 @@
 
 
 def blocks_kernel(lookup, left, hidden, right, copies, window, staged):
-    fill_copies(lookup, hidden.shape[0], (left, hidden, right), window, staged, copies)
+    fill_copies(lookup, hidden.shape[0], 0, (left, hidden, right), window, staged, copies)
 
 
 def vmem_specs(count):
@@ -198,7 +200,7 @@
     scale, terms, features, active, hidden, grad, hid_source, weight_source, grad_source, weight_t_source,
     outputs, input_grad, result,
     hid_copies, weight, grad_copies, weight_t, total,
-    r0, r1, r2, r3, r4, r5, local, send, recv,
+    own, r0, r1, r2, r3, r4, r5, arrive, local, send, recv,
 ):
     space, scene = lax.axis_index("space"), lax.axis_index("scene")
     core, x = scene % 2, scene // 2
@@ -220,7 +222,6 @@
         ((hid_source, hid_copies), (weight_source, weight), (grad_source, grad_copies), (weight_t_source, weight_t))
     ):
         moves.append(pltpu.make_async_copy(source, target, local.at[n]))
-        moves[n].start()
 
     def convolve(n):
         task, part = n // 3, n % 3
@@ -242,12 +243,12 @@
             summed = (features[b].astype(jnp.float32) + total[...]) * active[b]
             outputs[b] = summed.astype(jnp.bfloat16)
         elif part == 2:
-            kept = jnp.where(hidden[b].astype(jnp.float32) > 0, total[...], 0.0)
-            input_grad[b] = (grad[b].astype(jnp.float32) + kept).astype(jnp.bfloat16)
+            passed = jnp.where(hidden[b].astype(jnp.float32) > 0, total[...], 0.0)
+            input_grad[b] = (grad[b].astype(jnp.float32) + passed).astype(jnp.bfloat16)
 
     bricks = features.shape[0]
     chunks = r0.shape[0]
-    copies = {}
+    copies, kept = {}, {}
 
     def begin(stage, k, source, target, axis):
         copy = pltpu.make_async_remote_copy(
@@ -262,10 +263,13 @@
         x_first = k % 2 == 0
         if stage == 0:
             begin(0, k, terms.at[taps, :, :, :, :, 1 - core], r0.at[k], "core")
+            kept[k] = pltpu.make_async_copy(terms.at[taps, :, :, :, :, core], own.at[k], arrive.at[k])
+            kept[k].start()
             return
         copies[stage - 1, k].wait_recv()
         if stage == 1:
-            r0[k] = r0[k] + terms[taps, :, :, :, :, core]
+            kept[k].wait()
+            r0[k] = r0[k] + own[k]
             if x_first:
                 begin(1, k, r0.at[k, :, 1 - x], r1.at[k], "x")
             else:
@@ -297,6 +301,8 @@
     ahead = 2
     for k in range(min(ahead, chunks)):
         advance(0, k)
+    for move in moves:
+        move.start()
     parts = 6 * bricks
     for at in range(chunks + 5 * LAG):
         if at + ahead < chunks:
@@ -305,9 +311,9 @@
             k = at - LAG * (stage - 1)
             if 0 <= k < chunks:
                 advance(stage, k)
-        if 1 <= at <= parts:
-            convolve(at - 1)
-    for n in range(chunks + 5 * LAG - 1, parts):
+        if DELAY <= at < DELAY + parts:
+            convolve(at - DELAY)
+    for n in range(chunks + 5 * LAG - DELAY, parts):
         convolve(n)
     for copy in copies.values():
         copy.wait_send()
@@ -327,17 +333,19 @@
             jax.ShapeDtypeStruct(features.shape, jnp.bfloat16),
             jax.ShapeDtypeStruct((taps, 2 * rows, half // 2), f32),
         ),
-        in_specs=vmem_specs(5) + [pl.BlockSpec(memory_space=pl.ANY)] * 4,
+        in_specs=[pl.BlockSpec(memory_space=pl.ANY)] + vmem_specs(4) + [pl.BlockSpec(memory_space=pl.ANY)] * 4,
         out_specs=tuple(vmem_specs(3)),
         scratch_shapes=[pltpu.VMEM(array.shape, array.dtype) for array in streamed]
         + [
             pltpu.VMEM(features.shape[1:], f32),
+            pltpu.VMEM((chunks, GROUP, 2, 2, 2, 2) + tail, f32),
             pltpu.VMEM((chunks, GROUP, 2, 2, 2, 2) + tail, f32),
             pltpu.VMEM((chunks, GROUP, 2, 2, 2) + tail, f32),
             pltpu.VMEM((chunks, GROUP, 2, 2) + tail, f32),
             pltpu.VMEM((chunks, GROUP, 2) + tail, f32),
             pltpu.VMEM((chunks, GROUP) + tail, f32),
             pltpu.VMEM((chunks, GROUP) + tail, f32),
+            pltpu.SemaphoreType.DMA((chunks,)),
             pltpu.SemaphoreType.DMA((4,)),
             pltpu.SemaphoreType.DMA((6, chunks)),
             pltpu.SemaphoreType.DMA((6, chunks)),
@@ -388,19 +396,18 @@
     slot_live = (jnp.arange(bricks, dtype=jnp.int32) < counts[0, 0]).astype(jnp.int32)
     active = (occupancy[0] * slot_live[:, None]).reshape(bricks, voxels, 1)
     live = active.astype(jnp.float32)
-    hidden, grad, packed_hidden, packed_grad = prepare(
+    hidden, grad, packed = prepare(
         feats, cotangent.reshape(bricks, voxels, channels), live
     )
-    grad_left, grad_right = both_sides(packed_grad)
-    hid_left, hid_right = both_sides(packed_hidden)
+    left, right = both_sides(packed)
     first_id = (lax.axis_index("space") - 1) * bricks
     linked = neighbours[0]
     local_ids = jnp.where(linked >= 0, linked - first_id, -1)
     centre = (bricks + jnp.arange(bricks, dtype=jnp.int32))[:, None]
     lookup = jnp.concatenate([local_ids[:, :13], centre, local_ids[:, 13:]], axis=1)
     weight_t = weight[::-1].swapaxes(1, 2).reshape(9, 3 * channels, channels)
-    terms, grad_copies = gradient_terms(lookup, hidden.swapaxes(1, 2), (grad_left, grad, grad_right))
-    hid_copies = halo_blocks(lookup, (hid_left, hidden, hid_right))
+    terms, grad_copies = gradient_terms(lookup, hidden.swapaxes(1, 2), (left, grad, right))
+    hid_copies = halo_blocks(lookup, (left, hidden, right))
     fields = (feats, live, hidden, grad)
     streamed = (hid_copies, weight.reshape(9, 3 * channels, channels), grad_copies, weight_t)
     space, scene = lax.axis_size("space"), lax.axis_size("scene")

time: 121 us -> 121 us (level)
  waiting for transfers between devices: 12.2 us -> 18.3 us
  starting transfers between devices: 12.8 us -> 6.73 us
    ppermute x2 -> x1, starting transfers between devices: 10.3 us -> 5.45 us  [both_sides(): left = lax.ppermute(cells, 'space', [(i, i + 1) for i in range(ends)])]
    ppermute x2 -> x1, waiting for transfers between devices: 0.01 us -> 3.38 us  [both_sides(): right = lax.ppermute(cells, 'space', [(i + 1, i) for i in range(ends)])]
    ppermute x2 -> x1, waiting for transfers between devices: 12.2 us -> 14.9 us  [both_sides(): left = lax.ppermute(cells, 'space', [(i, i + 1) for i in range(ends)])]
    ppermute x2 -> x1, starting transfers between devices: 2.56 us -> 1.28 us  [both_sides(): right = lax.ppermute(cells, 'space', [(i + 1, i) for i in range(ends)])]
  transfers between devices with their start and end apart: 4 -> 2, of which waited for: 1 -> 2; matrix products, arithmetic and copies ran while one was open for 7% -> 7% of each run, Pallas kernels for 5% -> 0%
where the time goes in v4:
time: 121 us
  Pallas kernels  78.5 us (65%)
  waiting for transfers between devices  18.3 us (15%)
  local copies, waits for them, and re-layouts  14.4 us (12%)
  starting transfers between devices  6.73 us (6%)
  other arithmetic  1.55 us (1%)
  between operations  1.33 us (1%)
    pallas_call x1, Pallas kernels, scatter_sum(): pl.pallas_call(functools.partial(scatter_kernel, scale), out_shape=(jax.S...  52.8 us
    ppermute x1, waiting for transfers between devices, both_sides(): left = lax.ppermute(cells, 'space', [(i, i + 1) for i in range(ends)])  14.9 us
    pallas_call x1, Pallas kernels, gradient_terms(): pl.pallas_call(gradient_kernel, out_shape=(jax.ShapeDtypeStruct((27, 2, c...  13.9 us
    pallas_call x1, Pallas kernels, halo_blocks(): pl.pallas_call(blocks_kernel, out_shape=jax.ShapeDtypeStruct((3, bricks,...  6.7 us
    transpose x2, local copies, waits for them, and re-layouts, per_device(): weight_t = weight[::-1].swapaxes(1, 2).reshape(9, 3 * channels, channels)  5.81 us
    unnamed x5, local copies, waits for them, and re-layouts  5.57 us
    ppermute x1, starting transfers between devices, both_sides(): left = lax.ppermute(cells, 'space', [(i, i + 1) for i in range(ends)])  5.45 us
    pallas_call x1, Pallas kernels, prepare(): pl.pallas_call(prepare_kernel, out_shape=(whole, whole, surface), in_spec...  5.11 us
  transfers between devices with their start and end apart: 2, of which 2 were waited for; matrix products, arithmetic and copies ran while one was open for 7% of the time, Pallas kernels for 0%

profile of v4, /device:TPU:1, one launch (start us, length us, event | category | flops | bytes accessed | tf_op | source)
XLA Modules:
  0.0 120.8 jit_solution(2000047858709116638)
XLA Ops:
  1.3 0.9 copy.14
  2.2 0.9 multiply_convert_fusion.active
  3.1 5.1 %shard_map.85 = (bf16[2,512,256]{2,1,0:T(8,128)(2,1)}, bf16[2,512,256]{2,1,0:T(8,128)(2,1)}, bf16[4,320,256]{2,1,0:T(8,128)(2,1)}) custom-call(bf16[2,512,256]{2,1,0:T(8,128)(2,1)} %bitcast.18, bf16[2,512,256]{2,1,0:T(8,128)(2,1)} %bitcast.20, f32[2,512,1]{2,1,0:T(8,128)} %multiply_convert_fusion.active), custom_call_target="tpu_custom_call" | custom-call | tf_op jit(solution)/shard_map/pallas_call | solution.py:71
  8.2 1.3 %collective-permute-start.1 = (bf16[4,320,256]{2,1,0:T(8,128)(2,1)}, bf16[4,320,256]{2,1,0:T(8,128)(2,1)}, u32[]{:S(2)}, u32[]{:S(2)}) collective-permute-start(bf16[4,320,256]{2,1,0:T(8,128)(2,1)} %get-tuple-element.12), channel_id=1, source_target_pairs={{4,0},{8,4},{12,8},{16,12},{20,16},{24,20},{28,24},{5,1},{9,5},{13... | collective-permute-start | bytes 1966088 | tf_op jit(solution)/shard_map/ppermute | solution.py:21
  9.5 5.5 %collective-permute-start = (bf16[4,320,256]{2,1,0:T(8,128)(2,1)}, bf16[4,320,256]{2,1,0:T(8,128)(2,1)}, u32[]{:S(2)}, u32[]{:S(2)}) collective-permute-start(bf16[4,320,256]{2,1,0:T(8,128)(2,1)} %get-tuple-element.12), channel_id=1, source_target_pairs={{0,4},{4,8},{8,12},{12,16},{16,20},{20,24},{24,28},{1,5},{5,9},{9,... | collective-permute-start | bytes 1966088 | tf_op jit(solution)/shard_map/ppermute | solution.py:20
  15.0 2.0 %copy.16 = bf16[2,512,256]{1,2,0:T(8,128)(2,1)} copy(bf16[2,512,256]{2,1,0:T(8,128)(2,1)} %get-tuple-element.11.hidden) | data formatting | bytes 1048576 | tf_op jit(solution)/shard_map/pallas_call | solution.py:71
  17.0 2.2 %reverse_bitcast_fusion = bf16[27,256,256]{1,2,0:T(8,128)(2,1)S(1)} fusion(bf16[27,256,256]{2,1,0:T(8,128)(2,1)} %param.8), kind=kLoop, calls=%fused_computation | loop fusion | bytes 7077888 | tf_op jit(solution)/shard_map/transpose | solution.py:408
  19.2 0.0 copy-start
  19.2 3.6 %copy.17 = bf16[27,256,256]{2,1,0:T(8,128)(2,1)} copy(bf16[27,256,256]{1,2,0:T(8,128)(2,1)S(1)} %reverse_bitcast_fusion) | data formatting | bytes 7077888 | tf_op jit(solution)/shard_map/transpose | solution.py:408
  22.8 0.0 copy-done
  22.8 0.1 fusion.1
  22.9 0.6 pad_add_fusion.lookup
  23.6 3.4 %collective-permute-done.1.right = bf16[4,320,256]{2,1,0:T(8,128)(2,1)} collective-permute-done((bf16[4,320,256]{2,1,0:T(8,128)(2,1)}, bf16[4,320,256]{2,1,0:T(8,128)(2,1)}, u32[]{:S(2)}, u32[]{:S(2)}) %collective-permute-start.1) | collective-permute-done | bytes 655392 | tf_op jit(solution)/shard_map/ppermute | solution.py:21
  26.9 14.9 %collective-permute-done.left = bf16[4,320,256]{2,1,0:T(8,128)(2,1)} collective-permute-done((bf16[4,320,256]{2,1,0:T(8,128)(2,1)}, bf16[4,320,256]{2,1,0:T(8,128)(2,1)}, u32[]{:S(2)}, u32[]{:S(2)}) %collective-permute-start) | collective-permute-done | bytes 655392 | tf_op jit(solution)/shard_map/ppermute | solution.py:20
  41.9 6.7 %shard_map.87.hid_source = bf16[3,2,640,768]{3,2,1,0:T(8,128)(2,1)} custom-call(s32[2,27]{1,0:T(2,128)} %pad_add_fusion.lookup, bf16[4,320,256]{2,1,0:T(8,128)(2,1)} %collective-permute-done.left, bf16[2,512,256]{2,1,0:T(8,128)(2,1)} %get-tuple-element.11.hidden, bf16[4,320,256]{2,1,0:T(8,128)(2,1)} %collective-permute-done.1.right), custom_call_target="tpu_custom_call" | custom-call | bytes 30000000 | tf_op jit(solution)/shard_map/pallas_call | solution.py:188
  48.6 13.9 %shard_map.86 = (f32[27,2,256,128]{3,2,1,0:T(8,128)}, bf16[3,2,640,768]{3,2,1,0:T(8,128)(2,1)}) custom-call(s32[2,27]{1,0:T(2,128)} %pad_add_fusion.lookup, bf16[2,256,512]{2,1,0:T(8,128)(2,1)} %bitcast.21, bf16[4,320,256]{2,1,0:T(8,128)(2,1)} %collective-permute-done.left, bf16[2,512,256]{2,1,0:T(8,128)(2,1)} %get-tuple-element.13.grad, ...), custom_call_target="tpu_custom_call" | custom-call | flops 3623878656 | bytes 60000000 | tf_op jit(solution)/shard_map/pallas_call | solution.py:170
  62.4 52.8 %shard_map.88 = (bf16[2,512,256]{2,1,0:T(8,128)(2,1)}, bf16[2,512,256]{2,1,0:T(8,128)(2,1)}, f32[27,32,64]{2,1,0:T(8,128)}) custom-call(f32[27,2,2,2,2,2,16,128]{7,6,5,4,3,2,1,0:T(8,128)} %bitcast.17, bf16[2,512,256]{2,1,0:T(8,128)(2,1)} %bitcast.19, f32[2,512,1]{2,1,0:T(8,128)} %multiply_convert_fusion.active, ...), custom_call_target="tpu_custom_call" | custom-call | tf_op jit(solution)/shard_map/pallas_call | solution.py:329
  115.3 1.9 %copy.22 = bf16[1,2,8,8,8,256]{5,4,3,2,1,0:T(8,128)(2,1)} copy(bf16[1,2,8,8,8,256]{5,4,3,2,1,0:T(8,128)(2,1)} %bitcast.23) | data formatting | bytes 1048576
  117.2 1.9 %copy.23 = bf16[1,2,8,8,8,256]{5,4,3,2,1,0:T(8,128)(2,1)} copy(bf16[1,2,8,8,8,256]{5,4,3,2,1,0:T(8,128)(2,1)} %bitcast.22) | data formatting | bytes 1048576
  119.0 1.8 %copy.24 = f32[27,32,64]{2,1,0:T(8,128)} copy(f32[27,32,64]{2,1,0:T(8,128)} %get-tuple-element.26) | data formatting | bytes 442368
  (3 shorter events, 0.0 us)
Async XLA Ops:
  8.2 18.7 %collective-permute-start.1 = (bf16[4,320,256]{2,1,0:T(8,128)(2,1)}, bf16[4,320,256]{2,1,0:T(8,128)(2,1)}, u32[]{:S(2)}, u32[]{:S(2)}) collective-permute-start(bf16[4,320,256]{2,1,0:T(8,128)(2,1)} %get-tuple-element.12), channel_id=1, source_target_pairs={{4,0},{8,4},{12,8},{16,12},{20,16},{24,20},{28,24},{5,1},{9,5},{13... | collective-permute-start | bytes 1966088 | tf_op jit(solution)/shard_map/ppermute | solution.py:21
  9.5 32.4 %collective-permute-start = (bf16[4,320,256]{2,1,0:T(8,128)(2,1)}, bf16[4,320,256]{2,1,0:T(8,128)(2,1)}, u32[]{:S(2)}, u32[]{:S(2)}) collective-permute-start(bf16[4,320,256]{2,1,0:T(8,128)(2,1)} %get-tuple-element.12), channel_id=1, source_target_pairs={{0,4},{4,8},{8,12},{12,16},{16,20},{20,24},{24,28},{1,5},{5,9},{9,... | collective-permute-start | bytes 1966088 | tf_op jit(solution)/shard_map/ppermute | solution.py:20
  19.2 3.6 %copy-start = (s32[1,2,26]{2,1,0:T(2,128)S(1)}, s32[1,2,26]{2,1,0:T(2,128)}, u32[]{:S(2)}) copy-start(s32[1,2,26]{2,1,0:T(2,128)} %param.10) | copy-start | bytes 628

commit v5 on v3

--- a/solution.py
+++ b/solution.py
@@ -10,7 +10,7 @@
 MESH = pl.DeviceIdType.MESH
 VMEM_BYTES = 56 * 1024 * 1024
 GROUP = 3
-LAG = 2
+LAG = 3
 
 
 def both_sides(cells):

time: 121 us -> 122 us (level); the launches traced: 120 us -> 120 us
  no operation moved by 1% of the time
where the time goes in v5:
time: 122 us; the launch traced here: 120 us
  Pallas kernels  77.3 us (63%)
  local copies, waits for them, and re-layouts  14.4 us (12%)
  starting transfers between devices  12.8 us (10%)
  waiting for transfers between devices  12.2 us (10%)
  other arithmetic  1.58 us (1%)
  between operations  1.34 us (1%)
    pallas_call x1, Pallas kernels, scatter_sum(): pl.pallas_call(functools.partial(scatter_kernel, scale), out_shape=(jax.S...  52 us
    pallas_call x1, Pallas kernels, gradient_terms(): pl.pallas_call(gradient_kernel, out_shape=(jax.ShapeDtypeStruct((27, 2, c...  13.7 us
    ppermute x2, waiting for transfers between devices, both_sides(): left = lax.ppermute(cells, 'space', [(i, i + 1) for i in range(ends)])  12.2 us
    ppermute x2, starting transfers between devices, both_sides(): left = lax.ppermute(cells, 'space', [(i, i + 1) for i in range(ends)])  10.3 us
    pallas_call x1, Pallas kernels, halo_blocks(): pl.pallas_call(blocks_kernel, out_shape=jax.ShapeDtypeStruct((3, bricks,...  6.51 us
    transpose x2, local copies, waits for them, and re-layouts, per_device(): weight_t = weight[::-1].swapaxes(1, 2).reshape(9, 3 * channels, channels)  5.79 us
    unnamed x5, local copies, waits for them, and re-layouts  5.57 us
    pallas_call x1, Pallas kernels, prepare(): pl.pallas_call(prepare_kernel, out_shape=(whole, whole, surface, surface)...  5.11 us
  transfers between devices with their start and end apart: 4, of which 1 were waited for; matrix products, arithmetic and copies ran while one was open for 7% of the time, Pallas kernels for 5%

profile of v5, /device:TPU:1, one launch (start us, length us, event | category | flops | bytes accessed | tf_op | source)
XLA Modules:
  0.0 119.6 jit_solution(18025418021670098521)
XLA Ops:
  1.3 0.9 copy.14
  2.2 0.9 multiply_convert_fusion.active
  3.1 5.1 %shard_map.85 = (bf16[2,512,256]{2,1,0:T(8,128)(2,1)}, bf16[2,512,256]{2,1,0:T(8,128)(2,1)}, bf16[2,320,256]{2,1,0:T(8,128)(2,1)}, bf16[2,320,256]{2,1,0:T(8,128)(2,1)}) custom-call(bf16[2,512,256]{2,1,0:T(8,128)(2,1)} %bitcast.18, bf16[2,512,256]{2,1,0:T(8,128)(2,1)} %bitcast.20, f32[2,512,1]{2,1,0:T(8,128)} %multiply_convert_fusion.active), custom_call_target="tpu_custom_call" | custom-call | tf_op jit(solution)/shard_map/pallas_call | solution.py:69
  8.2 1.3 %collective-permute-start.1 = (bf16[2,320,256]{2,1,0:T(8,128)(2,1)}, bf16[2,320,256]{2,1,0:T(8,128)(2,1)}, u32[]{:S(2)}, u32[]{:S(2)}) collective-permute-start(bf16[2,320,256]{2,1,0:T(8,128)(2,1)} %get-tuple-element.13), channel_id=1, source_target_pairs={{4,0},{8,4},{12,8},{16,12},{20,16},{24,20},{28,24},{5,1},{9,5},{13... | collective-permute-start | bytes 983048 | tf_op jit(solution)/shard_map/ppermute | solution.py:20
  9.5 5.3 %collective-permute-start = (bf16[2,320,256]{2,1,0:T(8,128)(2,1)}, bf16[2,320,256]{2,1,0:T(8,128)(2,1)}, u32[]{:S(2)}, u32[]{:S(2)}) collective-permute-start(bf16[2,320,256]{2,1,0:T(8,128)(2,1)} %get-tuple-element.13), channel_id=1, source_target_pairs={{0,4},{4,8},{8,12},{12,16},{16,20},{20,24},{24,28},{1,5},{5,9},{9,... | collective-permute-start | bytes 983048 | tf_op jit(solution)/shard_map/ppermute | solution.py:19
  14.8 1.3 %collective-permute-start.3 = (bf16[2,320,256]{2,1,0:T(8,128)(2,1)}, bf16[2,320,256]{2,1,0:T(8,128)(2,1)}, u32[]{:S(2)}, u32[]{:S(2)}) collective-permute-start(bf16[2,320,256]{2,1,0:T(8,128)(2,1)} %get-tuple-element.16), channel_id=1, source_target_pairs={{4,0},{8,4},{12,8},{16,12},{20,16},{24,20},{28,24},{5,1},{9,5},{13... | collective-permute-start | bytes 983048 | tf_op jit(solution)/shard_map/ppermute | solution.py:20
  16.1 4.9 %collective-permute-start.2 = (bf16[2,320,256]{2,1,0:T(8,128)(2,1)}, bf16[2,320,256]{2,1,0:T(8,128)(2,1)}, u32[]{:S(2)}, u32[]{:S(2)}) collective-permute-start(bf16[2,320,256]{2,1,0:T(8,128)(2,1)} %get-tuple-element.16), channel_id=1, source_target_pairs={{0,4},{4,8},{8,12},{12,16},{16,20},{20,24},{24,28},{1,5},{5,9},{9,... | collective-permute-start | bytes 983048 | tf_op jit(solution)/shard_map/ppermute | solution.py:19
  21.1 2.1 %copy.16 = bf16[2,512,256]{1,2,0:T(8,128)(2,1)} copy(bf16[2,512,256]{2,1,0:T(8,128)(2,1)} %get-tuple-element.12.hidden) | data formatting | bytes 1048576 | tf_op jit(solution)/shard_map/pallas_call | solution.py:69
  23.1 2.2 %reverse_bitcast_fusion = bf16[27,256,256]{1,2,0:T(8,128)(2,1)S(1)} fusion(bf16[27,256,256]{2,1,0:T(8,128)(2,1)} %param.8), kind=kLoop, calls=%fused_computation | loop fusion | bytes 7077888 | tf_op jit(solution)/shard_map/transpose | solution.py:401
  25.4 0.0 copy-start
  25.4 3.6 %copy.17 = bf16[27,256,256]{2,1,0:T(8,128)(2,1)} copy(bf16[27,256,256]{1,2,0:T(8,128)(2,1)S(1)} %reverse_bitcast_fusion) | data formatting | bytes 7077888 | tf_op jit(solution)/shard_map/transpose | solution.py:401
  28.9 0.0 copy-done
  28.9 0.1 fusion.1
  29.0 0.7 pad_add_fusion.lookup
  29.7 0.0 collective-permute-done.3.right
  29.7 12.2 %collective-permute-done.2.left = bf16[2,320,256]{2,1,0:T(8,128)(2,1)} collective-permute-done((bf16[2,320,256]{2,1,0:T(8,128)(2,1)}, bf16[2,320,256]{2,1,0:T(8,128)(2,1)}, u32[]{:S(2)}, u32[]{:S(2)}) %collective-permute-start.2) | collective-permute-done | bytes 327712 | tf_op jit(solution)/shard_map/ppermute | solution.py:19
  41.9 6.5 %shard_map.87.hid_source = bf16[3,2,640,768]{3,2,1,0:T(8,128)(2,1)} custom-call(s32[2,27]{1,0:T(2,128)} %pad_add_fusion.lookup, bf16[2,320,256]{2,1,0:T(8,128)(2,1)} %collective-permute-done.2.left, bf16[2,512,256]{2,1,0:T(8,128)(2,1)} %get-tuple-element.12.hidden, bf16[2,320,256]{2,1,0:T(8,128)(2,1)} %collective-permute-done.3.right), custom_call_target="tpu_custom_call" | custom-call | bytes 30000000 | tf_op jit(solution)/shard_map/pallas_call | solution.py:186
  48.4 0.0 collective-permute-done.1.right
  48.4 0.0 collective-permute-done.left
  48.4 13.7 %shard_map.86 = (f32[27,2,256,128]{3,2,1,0:T(8,128)}, bf16[3,2,640,768]{3,2,1,0:T(8,128)(2,1)}) custom-call(s32[2,27]{1,0:T(2,128)} %pad_add_fusion.lookup, bf16[2,256,512]{2,1,0:T(8,128)(2,1)} %bitcast.21, bf16[2,320,256]{2,1,0:T(8,128)(2,1)} %collective-permute-done.left, bf16[2,512,256]{2,1,0:T(8,128)(2,1)} %get-tuple-element.14.grad, ...), custom_call_target="tpu_custom_call" | custom-call | flops 3623878656 | bytes 60000000 | tf_op jit(solution)/shard_map/pallas_call | solution.py:168
  62.1 52.0 %shard_map.88 = (bf16[2,512,256]{2,1,0:T(8,128)(2,1)}, bf16[2,512,256]{2,1,0:T(8,128)(2,1)}, f32[27,32,64]{2,1,0:T(8,128)}) custom-call(f32[27,2,2,2,2,2,16,128]{7,6,5,4,3,2,1,0:T(8,128)} %bitcast.17, bf16[2,512,256]{2,1,0:T(8,128)(2,1)} %bitcast.19, f32[2,512,1]{2,1,0:T(8,128)} %multiply_convert_fusion.active, ...), custom_call_target="tpu_custom_call" | custom-call | tf_op jit(solution)/shard_map/pallas_call | solution.py:323
  114.1 1.9 %copy.22 = bf16[1,2,8,8,8,256]{5,4,3,2,1,0:T(8,128)(2,1)} copy(bf16[1,2,8,8,8,256]{5,4,3,2,1,0:T(8,128)(2,1)} %bitcast.23) | data formatting | bytes 1048576
  116.0 1.9 %copy.23 = bf16[1,2,8,8,8,256]{5,4,3,2,1,0:T(8,128)(2,1)} copy(bf16[1,2,8,8,8,256]{5,4,3,2,1,0:T(8,128)(2,1)} %bitcast.22) | data formatting | bytes 1048576
  117.8 1.8 %copy.24 = f32[27,32,64]{2,1,0:T(8,128)} copy(f32[27,32,64]{2,1,0:T(8,128)} %get-tuple-element.28) | data formatting | bytes 442368
  (3 shorter events, 0.0 us)
Async XLA Ops:
  8.2 40.2 %collective-permute-start.1 = (bf16[2,320,256]{2,1,0:T(8,128)(2,1)}, bf16[2,320,256]{2,1,0:T(8,128)(2,1)}, u32[]{:S(2)}, u32[]{:S(2)}) collective-permute-start(bf16[2,320,256]{2,1,0:T(8,128)(2,1)} %get-tuple-element.13), channel_id=1, source_target_pairs={{4,0},{8,4},{12,8},{16,12},{20,16},{24,20},{28,24},{5,1},{9,5},{13... | collective-permute-start | bytes 983048 | tf_op jit(solution)/shard_map/ppermute | solution.py:20
  9.5 38.9 %collective-permute-start = (bf16[2,320,256]{2,1,0:T(8,128)(2,1)}, bf16[2,320,256]{2,1,0:T(8,128)(2,1)}, u32[]{:S(2)}, u32[]{:S(2)}) collective-permute-start(bf16[2,320,256]{2,1,0:T(8,128)(2,1)} %get-tuple-element.13), channel_id=1, source_target_pairs={{0,4},{4,8},{8,12},{12,16},{16,20},{20,24},{24,28},{1,5},{5,9},{9,... | collective-permute-start | bytes 983048 | tf_op jit(solution)/shard_map/ppermute | solution.py:19
  14.8 14.8 %collective-permute-start.3 = (bf16[2,320,256]{2,1,0:T(8,128)(2,1)}, bf16[2,320,256]{2,1,0:T(8,128)(2,1)}, u32[]{:S(2)}, u32[]{:S(2)}) collective-permute-start(bf16[2,320,256]{2,1,0:T(8,128)(2,1)} %get-tuple-element.16), channel_id=1, source_target_pairs={{4,0},{8,4},{12,8},{16,12},{20,16},{24,20},{28,24},{5,1},{9,5},{13... | collective-permute-start | bytes 983048 | tf_op jit(solution)/shard_map/ppermute | solution.py:20
  16.1 25.7 %collective-permute-start.2 = (bf16[2,320,256]{2,1,0:T(8,128)(2,1)}, bf16[2,320,256]{2,1,0:T(8,128)(2,1)}, u32[]{:S(2)}, u32[]{:S(2)}) collective-permute-start(bf16[2,320,256]{2,1,0:T(8,128)(2,1)} %get-tuple-element.16), channel_id=1, source_target_pairs={{0,4},{4,8},{8,12},{12,16},{16,20},{20,24},{24,28},{1,5},{5,9},{9,... | collective-permute-start | bytes 983048 | tf_op jit(solution)/shard_map/ppermute | solution.py:19
  25.4 3.6 %copy-start = (s32[1,2,26]{2,1,0:T(2,128)S(1)}, s32[1,2,26]{2,1,0:T(2,128)}, u32[]{:S(2)}) copy-start(s32[1,2,26]{2,1,0:T(2,128)} %param.10) | copy-start | bytes 628
